TPU v7x, 128 devices: a whole 4x4x4 slice. The times are simulated.
128 devices in a mesh: dp: 32 (over x_lo, y, z), tensor: 4 (over x_hi, core).
Axes of the slice: x: 4 (x_hi: 2, x_lo: 2; x = x_hi * 2 + x_lo), y: 4, z: 4, core: 2. Of those that a mesh axis runs over, the one named last changes fastest.
Arguments:
- tokens: bfloat16 [8192, 1024], P('dp')
- segments: int32 [8192], P('dp'), may hold values from 0 to 4, as said below
- routes: int32 [8192], P('dp'), may hold values from 0 to 1, as said below
- slot_table: int32 [32, 2, 128], P('dp'), may hold values from 0 to 256, as said below
- ln_gain: bfloat16 [1024], replicated, may hold values from 0.5 to 1.5
- ln_shift: bfloat16 [1024], replicated, may hold values from -1 to 1
- qkv_proj: bfloat16 [3, 1024, 1024], P(None, None, 'tensor'), may hold values from -0.25 to 0.25
- qv_bias: bfloat16 [2, 1024], P(None, 'tensor'), may hold values from -1.5 to 1.5
- out_proj: bfloat16 [1024, 1024], P('tensor'), may hold values from -0.375 to 0.375
- out_bias: bfloat16 [1024], replicated, may hold values from -1 to 1
- centroids: bfloat16 [2, 1024], replicated, may hold values from -0.0625 to 0.0625
- ffn_gain: bfloat16 [2, 2, 1024], replicated, may hold values from 0.5 to 1.5
- ffn_shift: bfloat16 [2, 2, 1024], replicated, may hold values from -1 to 1
- up_proj: bfloat16 [2, 2, 1024, 4096], P(None, None, None, 'tensor'), may hold values from -0.1875 to 0.1875
- up_bias: bfloat16 [2, 2, 4096], P(None, None, 'tensor'), may hold values from -1 to 1
- down_proj: bfloat16 [2, 2, 4096, 1024], P(None, None, 'tensor'), may hold values from -0.125 to 0.125
- down_bias: bfloat16 [2, 2, 1024], replicated, may hold values from -0.5 to 0.5
- cotangent: bfloat16 [8192, 1024], P('dp'), may hold values from -6 to 6
Outputs:
- result: bfloat16 [8192, 1024], P('dp')
- tokens_grad: bfloat16 [8192, 1024], P('dp')
- ln_gain_grad: float32 [1024], P('dp')
- ln_shift_grad: float32 [1024], P('dp')
- qkv_proj_grad: float32 [3, 1024, 1024], P(None, 'dp', 'tensor')
- qv_bias_grad: float32 [2, 1024], P(None, 'tensor')
- out_proj_grad: float32 [1024, 1024], P('tensor', 'dp')
- out_bias_grad: float32 [1024], P('dp')
- centroids_grad: float32 [2, 1024], P(None, 'dp')
- ffn_gain_grad: float32 [2, 2, 1024], P(None, None, 'dp')
- ffn_shift_grad: float32 [2, 2, 1024], P(None, None, 'dp')
- up_proj_grad: float32 [2, 2, 1024, 4096], P(None, None, 'dp', 'tensor')
- up_bias_grad: float32 [2, 2, 4096], P(None, None, 'tensor')
- down_proj_grad: float32 [2, 2, 4096, 1024], P(None, None, 'tensor', 'dp')
- down_bias_grad: float32 [2, 2, 1024], P(None, None, 'dp')
- rms_values: float32 [4], replicated
Inputs may be any that keep to these rules, and one draw needn't show every extreme that they name: `segments`: within each pack of 256 tokens the valid tokens come first, numbered from 1 upward and never falling; the rest of the pack is padding, numbered 0. The share of valid tokens falls along the packs from nearly all of the first to about a third of the last. A pack holds at most 4 documents, and the first pack holds 4. `routes`: the route of a valid token is the expert of its slot; that of padding is arbitrary. slot_table[p, e, c] is the position within pack p of the c-th valid token of that pack routed to e, in order of position, or 256 where fewer tokens are routed to e; every valid token stands in exactly one slot, padding in none; in the first pack one expert fills all 128 slots.
All inputs are finite; a program needn't handle non-finite values.
Results may differ from a plain program's by a relative error of at most 0.014.
The roundings to bfloat16 on the way count: a program that leaves them out, or rounds other values in their place, can miss the bound.
Values sent between devices are 32-bit elements; how exact they have to be, the bound alone decides.
A program may use at most 256 MiB of HBM per device.

v0:
```python
import math

import jax
import jax.numpy as jnp
from jax import lax
from jax.sharding import PartitionSpec as P

HD = 64


norm_eps = 1e-05
highest = lax.Precision.HIGHEST


def copy_for_each(x, axis):
    count = lax.axis_size(axis)
    return lax.all_to_all(jnp.broadcast_to(x[None], (count, *x.shape)), axis, 0, 0, tiled=True)


def taken_together(x, axis):
    everything = copy_for_each(x, axis)
    return jnp.sum(everything, axis=0)


def in_one_piece(arrays, axis, dim, along):
    widths = [math.prod(a.shape[along:]) for a in arrays]
    both = jnp.concatenate(
        [a.reshape(*a.shape[:along], w) for a, w in zip(arrays, widths)], axis=along
    )
    filled = lax.psum_scatter(both, axis, scatter_dimension=dim, tiled=True)
    pieces = jnp.split(filled, [sum(widths[:k]) for k in range(1, len(widths))], axis=along)
    return tuple(
        (b.reshape(*filled.shape[:along], *a.shape[along:]) for a, b in zip(arrays, pieces))
    )


def packed_total(arrays, axis):
    vector, at, done = (jnp.concatenate([a.reshape(-1) for a in arrays]), 0, [])
    running = taken_together(vector, axis)
    for a in arrays:
        done.append(running[at : at + a.size].reshape(a.shape))
        at += a.size
    return tuple(done)


def layer_norm(inputs, norm_gain, norm_shift):
    center = inputs - jnp.mean(inputs, axis=-1, keepdims=True)
    spread = jnp.mean(center * center, axis=-1, keepdims=True)
    return center * lax.rsqrt(spread + norm_eps) * norm_gain + norm_shift


def gelu_tanh(inputs):
    return jax.nn.gelu(inputs, approximate=True)


def product(left, right):
    return jnp.dot(left, right, preferred_element_type=jnp.float32)


def local(
    tokens,
    segments,
    routes,
    slot_table,
    ln_gain,
    ln_shift,
    qkv_proj,
    qv_bias,
    out_proj,
    out_bias,
    centroids,
    ffn_gain,
    ffn_shift,
    up_proj,
    up_bias,
    down_proj,
    down_bias,
    cotangent,
):
    length, model_width = tokens.shape
    experts, capacity = (slot_table.shape[1], slot_table.shape[2])
    local_heads = qkv_proj.shape[2] // HD
    score_scale = HD ** (-0.5)
    residual = tokens.astype(jnp.float32)
    is_valid = (segments != 0).astype(jnp.float32)
    position = jnp.arange(length, dtype=jnp.int32)
    normed, norm_pull = jax.vjp(
        layer_norm, residual, ln_gain.astype(jnp.float32), ln_shift.astype(jnp.float32)
    )
    normed_low = normed.astype(jnp.bfloat16)
    query_heads = (
        (product(normed_low, qkv_proj[0]) + qv_bias[0].astype(jnp.float32))
        .astype(jnp.bfloat16)
        .reshape(length, local_heads, HD)
    )
    keyed_heads = (
        product(normed_low, qkv_proj[1]).astype(jnp.bfloat16).reshape(length, local_heads, HD)
    )
    value_heads = (
        (product(normed_low, qkv_proj[2]) + qv_bias[1].astype(jnp.float32))
        .astype(jnp.bfloat16)
        .reshape(length, local_heads, HD)
    )
    allowed = (
        (segments[:, None] == segments[None, :])
        & (position[None, :] <= position[:, None])
        & (segments[:, None] != 0)
    )
    raw_scores = (
        jnp.einsum("qhd,khd->hqk", query_heads, keyed_heads, preferred_element_type=jnp.float32)
        * score_scale
    )
    masked = jnp.where(allowed[None], raw_scores, -1e30)
    row_top = jnp.max(masked, axis=-1, keepdims=True)
    exponent = jnp.where(allowed[None], jnp.exp(masked - row_top), 0.0)
    row_total = jnp.sum(exponent, axis=-1, keepdims=True) + (1.0 - is_valid)[None, :, None]
    attn_probs = exponent / row_total
    probs_low = attn_probs.astype(jnp.bfloat16)
    attn_mixed = jnp.einsum(
        "hqk,khd->qhd", probs_low, value_heads, preferred_element_type=jnp.float32
    )
    mixed_low = attn_mixed.reshape(length, local_heads * HD).astype(jnp.bfloat16)
    branch = taken_together(product(mixed_low, out_proj), "tensor") + out_bias.astype(jnp.float32)
    hidden = residual + branch
    cent_rows = centroids.astype(jnp.float32)
    route_hot = (routes[:, None] == jnp.arange(experts, dtype=jnp.int32)[None, :]).astype(
        jnp.float32
    )
    router_scores = jnp.dot(hidden, cent_rows.T, precision=highest)
    logits = jnp.sum(router_scores * route_hot, axis=1)
    gate_sigmoid = jax.nn.sigmoid(logits)
    gating = gate_sigmoid * is_valid
    flat_slots = slot_table.reshape(-1)
    filled = (flat_slots < length).astype(jnp.float32)
    safe_slots = jnp.minimum(flat_slots, length - 1)
    expert_rows = [hidden[safe_slots] * filled[:, None]]
    saved_parts = []
    for sublayer in range(2):
        current = expert_rows[sublayer].reshape(experts, capacity, model_width)
        normed_e, ffn_pull = jax.vjp(
            layer_norm,
            current,
            ffn_gain[:, sublayer].astype(jnp.float32)[:, None, :],
            ffn_shift[:, sublayer].astype(jnp.float32)[:, None, :],
        )
        normed_e_low = normed_e.astype(jnp.bfloat16)
        pre_act = (
            jnp.einsum(
                "ecd,edf->ecf",
                normed_e_low,
                up_proj[:, sublayer],
                preferred_element_type=jnp.float32,
            )
            + up_bias[:, sublayer].astype(jnp.float32)[:, None, :]
        )
        act_value, gelu_pull = jax.vjp(gelu_tanh, pre_act)
        act_low = act_value.astype(jnp.bfloat16)
        partial_out = jnp.einsum(
            "ecf,efd->ecd", act_low, down_proj[:, sublayer], preferred_element_type=jnp.float32
        )
        branch_out = (
            taken_together(partial_out, "tensor")
            + down_bias[:, sublayer].astype(jnp.float32)[:, None, :]
        )
        expert_rows.append((current + branch_out).reshape(experts * capacity, model_width))
        saved_parts.append((ffn_pull, normed_e_low, gelu_pull, act_low))
    combined = (
        jnp.zeros((length, model_width), jnp.float32)
        .at[flat_slots]
        .add(expert_rows[2], mode="drop")
    )
    result_value = hidden + gating[:, None] * combined
    result = result_value.astype(jnp.bfloat16)
    valid_col = is_valid[:, None]
    hidden_sq = jnp.sum(hidden * hidden * valid_col)
    first_sq = jnp.sum(expert_rows[1] * expert_rows[1] * filled[:, None])
    second_sq = jnp.sum(expert_rows[2] * expert_rows[2] * filled[:, None])
    result_sq = jnp.sum(result_value * result_value * valid_col)
    valid_count = jnp.sum(is_valid)
    grad_result = cotangent.astype(jnp.float32)
    grad_comb = gating[:, None] * grad_result
    grad_gate = jnp.sum(grad_result * combined, axis=1)
    grad_logit = grad_gate * gate_sigmoid * (1.0 - gate_sigmoid) * is_valid
    grad_hidden = grad_result + grad_logit[:, None] * jnp.dot(
        route_hot, cent_rows, precision=highest
    )
    centroid_local = jnp.dot(route_hot.T, grad_logit[:, None] * hidden, precision=highest)
    grad_rows = grad_comb[safe_slots] * filled[:, None]
    gain_parts = [None, None]
    shift_parts = [None, None]
    up_parts = [None, None]
    upbias_parts = [None, None]
    down_parts = [None, None]
    downbias_parts = [None, None]
    for sublayer in (1, 0):
        ffn_pull, normed_e_low, gelu_pull, act_low = saved_parts[sublayer]
        grad_out_low = grad_rows.reshape(experts, capacity, model_width).astype(jnp.bfloat16)
        downbias_parts[sublayer] = jnp.sum(grad_out_low, axis=1, dtype=jnp.float32)
        down_parts[sublayer] = jnp.einsum(
            "ecf,ecd->efd", act_low, grad_out_low, preferred_element_type=jnp.float32
        )
        grad_act = jnp.einsum(
            "ecd,efd->ecf", grad_out_low, down_proj[:, sublayer], preferred_element_type=jnp.float32
        )
        grad_pre_low = gelu_pull(grad_act)[0].astype(jnp.bfloat16)
        upbias_parts[sublayer] = jnp.sum(grad_pre_low, axis=1, dtype=jnp.float32)
        up_parts[sublayer] = jnp.einsum(
            "ecd,ecf->edf", normed_e_low, grad_pre_low, preferred_element_type=jnp.float32
        )
        grad_normed_part = jnp.einsum(
            "ecf,edf->ecd", grad_pre_low, up_proj[:, sublayer], preferred_element_type=jnp.float32
        )
        grad_normed_e = lax.psum(grad_normed_part, "tensor")
        grad_current, grad_gain_e, grad_shift_e = ffn_pull(grad_normed_e)
        gain_parts[sublayer] = grad_gain_e[:, 0]
        shift_parts[sublayer] = grad_shift_e[:, 0]
        grad_rows = grad_rows + grad_current.reshape(experts * capacity, model_width)
    gain_e_local = jnp.stack(gain_parts, axis=1)
    shift_e_local = jnp.stack(shift_parts, axis=1)
    up_local = jnp.stack(up_parts, axis=1)
    upbias_local = jnp.stack(upbias_parts, axis=1)
    down_local = jnp.stack(down_parts, axis=1)
    downbias_local = jnp.stack(downbias_parts, axis=1)
    grad_hidden = grad_hidden + jnp.zeros((length, model_width), jnp.float32).at[flat_slots].add(
        grad_rows, mode="drop"
    )
    grad_branch_low = grad_hidden.astype(jnp.bfloat16)
    outbias_local = jnp.sum(grad_branch_low, axis=0, dtype=jnp.float32)
    outproj_local = jnp.einsum(
        "th,td->hd", mixed_low, grad_branch_low, preferred_element_type=jnp.float32
    )
    grad_mixed = (
        jnp.einsum("td,hd->th", grad_branch_low, out_proj, preferred_element_type=jnp.float32)
        .astype(jnp.bfloat16)
        .reshape(length, local_heads, HD)
    )
    grad_probs = jnp.einsum(
        "qhd,khd->hqk", grad_mixed, value_heads, preferred_element_type=jnp.float32
    )
    grad_value = jnp.einsum(
        "hqk,qhd->khd", probs_low, grad_mixed, preferred_element_type=jnp.float32
    ).astype(jnp.bfloat16)
    row_dot = jnp.sum(attn_probs * grad_probs, axis=-1, keepdims=True)
    grad_scores = (attn_probs * (grad_probs - row_dot)).astype(jnp.bfloat16)
    grad_query = (
        jnp.einsum("hqk,khd->qhd", grad_scores, keyed_heads, preferred_element_type=jnp.float32)
        * score_scale
    ).astype(jnp.bfloat16)
    grad_keyed = (
        jnp.einsum("hqk,qhd->khd", grad_scores, query_heads, preferred_element_type=jnp.float32)
        * score_scale
    ).astype(jnp.bfloat16)
    grad_qkv = jnp.stack([grad_query, grad_keyed, grad_value]).reshape(3, length, local_heads * HD)
    qkv_local = jnp.einsum("td,sth->sdh", normed_low, grad_qkv, preferred_element_type=jnp.float32)
    qvbias_local = jnp.stack(
        [
            jnp.sum(grad_qkv[0], axis=0, dtype=jnp.float32),
            jnp.sum(grad_qkv[2], axis=0, dtype=jnp.float32),
        ]
    )
    grad_normed = taken_together(
        jnp.einsum("sth,sdh->td", grad_qkv, qkv_proj, preferred_element_type=jnp.float32), "tensor"
    )
    grad_residual, gain_local, shift_local = norm_pull(grad_normed)
    tokens_grad = (grad_hidden + grad_residual).astype(jnp.bfloat16)
    (
        ln_gain_grad,
        ln_shift_grad,
        qkv_proj_grad,
        out_proj_grad,
        out_bias_grad,
        centroids_grad,
        ffn_gain_grad,
        ffn_shift_grad,
        up_proj_grad,
        down_proj_grad,
        down_bias_grad,
    ) = (
        lax.psum_scatter(gain_local, "dp", scatter_dimension=0, tiled=True),
        lax.psum_scatter(shift_local, "dp", scatter_dimension=0, tiled=True),
        lax.psum_scatter(qkv_local, "dp", scatter_dimension=1, tiled=True),
        lax.psum_scatter(outproj_local, "dp", scatter_dimension=1, tiled=True),
        lax.psum_scatter(outbias_local, "dp", scatter_dimension=0, tiled=True),
        lax.psum_scatter(centroid_local, "dp", scatter_dimension=1, tiled=True),
        *in_one_piece((gain_e_local, shift_e_local, up_local), "dp", 2, 3),
        lax.psum_scatter(down_local, "dp", scatter_dimension=3, tiled=True),
        lax.psum_scatter(downbias_local, "dp", scatter_dimension=2, tiled=True),
    )
    merged = packed_total(
        (hidden_sq, first_sq, second_sq, result_sq, valid_count, qvbias_local, upbias_local), "dp"
    )
    totals = merged[:5]
    qv_bias_grad = merged[5]
    up_bias_grad = merged[6]
    rms_values = jnp.sqrt(
        jnp.stack([totals[0], totals[1], totals[2], totals[3]]) / (totals[4] * model_width)
    )
    return (
        result,
        tokens_grad,
        ln_gain_grad,
        ln_shift_grad,
        qkv_proj_grad,
        qv_bias_grad,
        out_proj_grad,
        out_bias_grad,
        centroids_grad,
        ffn_gain_grad,
        ffn_shift_grad,
        up_proj_grad,
        up_bias_grad,
        down_proj_grad,
        down_bias_grad,
        rms_values,
    )


def solution(mesh):
    return jax.shard_map(
        local,
        mesh=mesh,
        in_specs=(
            P("dp", None),
            P("dp"),
            P("dp"),
            P("dp", None, None),
            P(),
            P(),
            P(None, None, "tensor"),
            P(None, "tensor"),
            P("tensor", None),
            P(),
            P(),
            P(),
            P(),
            P(None, None, None, "tensor"),
            P(None, None, "tensor"),
            P(None, None, "tensor", None),
            P(),
            P("dp", None),
        ),
        out_specs=(
            P("dp", None),
            P("dp", None),
            P("dp"),
            P("dp"),
            P(None, "dp", "tensor"),
            P(None, "tensor"),
            P("tensor", "dp"),
            P("dp"),
            P(None, "dp"),
            P(None, None, "dp"),
            P(None, None, "dp"),
            P(None, None, "dp", "tensor"),
            P(None, None, "tensor"),
            P(None, None, "tensor", "dp"),
            P(None, None, "dp"),
            P(),
        ),
        check_vma=False,
    )
```

profile of v0, /device:TPU:1, one launch (start us, length us, event | category | flops | bytes accessed | tf_op | source)
XLA Modules:
  0.0 1357.7 jit_solution(9722348624509048537)
XLA Ops:
  25.4 6.2 all-to-all-start
  31.9 48.7 %all-to-all-done = f32[4,256,1024]{2,1,0:T(8,128)} async-done(((f32[4,256,1024]{2,1,0:T(8,128)}), f32[4,256,1024]{2,1,0:T(8,128)}, u32[]{:S(2)}, u32[]{:S(2)}) %all-to-all-start) | async-done | bytes 4194336 | tf_op jit(solution)/shard_map/all_to_all | solution.py:17
  95.0 5.7 all-to-all-start.1
  100.8 48.9 %all-to-all-done.1 = f32[4,2,128,1024]{3,2,1,0:T(8,128)} async-done(((f32[4,2,128,1024]{3,2,1,0:T(8,128)}), f32[4,2,128,1024]{3,2,1,0:T(8,128)}, u32[]{:S(2)}, u32[]{:S(2)}) %all-to-all-start.1) | async-done | bytes 4194336 | tf_op jit(solution)/shard_map/all_to_all | solution.py:17
  169.1 5.7 all-to-all-start.2
  175.7 48.0 %all-to-all-done.2 = f32[4,2,128,1024]{3,2,1,0:T(8,128)} async-done(((f32[4,2,128,1024]{3,2,1,0:T(8,128)}), f32[4,2,128,1024]{3,2,1,0:T(8,128)}, u32[]{:S(2)}, u32[]{:S(2)}) %all-to-all-start.2) | async-done | bytes 4194336 | tf_op jit(solution)/shard_map/all_to_all | solution.py:17
  246.1 5.0 convert_reduce_fusion.4
  251.9 4.7 fusion.5
  257.1 46.4 %all-reduce.13.cloned.1.call-done = f32[2,128,1024]{2,1,0:T(8,128)} async-done(((f32[2,128,1024]{2,1,0:T(8,128)}), f32[2,128,1024]{2,1,0:T(8,128)}) %all-reduce.13.cloned.1.call-update) | async-done | bytes 1048592 | tf_op jit(solution)/shard_map/psum | solution.py:213
  311.9 4.9 convert_reduce_fusion.5
  320.2 5.9 convolution_bitcast_fusion
  328.0 5.9 convolution_bitcast_fusion.1
  336.0 11.9 pad_maximum_fusion.1
  347.9 25.5 %copy.148 = f32[2,2,1024,1024]{2,1,0,3:T(2,128)} copy(f32[2,2,1024,1024]{3,2,0,1:T(8,128)} %pad_maximum_fusion.1) | data formatting | bytes 33554432 | tf_op jit(solution)/shard_map/stack | solution.py:222
  378.9 6.1 pad_maximum_fusion
  388.4 43.6 %concatenate.8 = f32[2,2,1024,1026]{2,3,0,1:T(8,128)} concatenate(f32[2,2,1024,1]{2,3,0,1:T(1,128)S(1)} %reshape.581, f32[2,2,1024,1]{2,3,0,1:T(1,128)S(1)} %reshape.584, f32[2,2,1024,1024]{2,3,0,1:T(8,128)} %pad_maximum_fusion), dimensions={3} | concatenate | bytes 33619968 | tf_op jit(solution)/shard_map/concatenate | solution.py:27
  432.0 27.8 %copy.143 = f32[2,2,1024,1026]{3,1,0,2:T(2,128)} copy(f32[2,2,1024,1026]{2,3,0,1:T(8,128)} %concatenate.8) | data formatting | bytes 33619968 | tf_op jit(solution)/shard_map/concatenate | solution.py:27
  475.2 5.0 copy.139
  485.7 7.2 all-to-all-start.4
  494.9 16.6 %all-to-all-done.4 = f32[32,1,4613]{2,1,0:T(1,128)} async-done(((f32[32,1,4613]{2,1,0:T(1,128)}), f32[32,1,4613]{2,1,0:T(1,128)}, u32[]{:S(2)}, u32[]{:S(2)}) %all-to-all-start.4) | async-done | bytes 590496 | tf_op jit(solution)/shard_map/all_to_all | solution.py:17
  514.0 5.8 all-to-all-start.3
  522.7 201.6 %reduce-scatter.12.cloned.1.call-done = f32[32,4]{1,0:T(8,128)} async-done(((f32[1024,4]{1,0:T(8,128)}), f32[32,4]{1,0:T(8,128)}) %reduce-scatter.12.cloned.1.call-update) | async-done | bytes 528
  736.8 139.8 %all-reduce.6 = (f32[1024]{0:T(1024)S(1)}, f32[1024]{0:T(1024)S(1)}, f32[1024]{0:T(1024)S(1)}) all-reduce(f32[1024]{0:T(1024)S(1)} %get-tuple-element.100, f32[1024]{0:T(1024)S(1)} %get-tuple-element.96, f32[1024]{0:T(1024)S(1)} %get-tuple-element.131), channel_id=2, replica_groups=mesh['dp'=32,'tensor'=4] {'dp'}, use_global_device_ids=true, to_apply=%region_26.27.clone | all-reduce | flops 3072 | bytes 24576
  880.5 462.8 %all-reduce.19.cloned.1.call-done = (f32[3,1024,256]{2,0,1:T(4,128)}, f32[2,2,1024,1026]{3,1,0,2:T(2,128)}) async-done(((f32[3,1024,256]{2,0,1:T(4,128)}, f32[2,2,1024,1026]{3,1,0,2:T(2,128)}), (f32[3,1024,256]{2,0,1:T(4,128)}, f32[2,2,1024,1026]{3,1,0,2:T(2,128)})) %all-reduce.19.cloned.1.call-update) | async-done | bytes 19955728
  (231 shorter events, 150.0 us)
Async XLA Ops:
  8.0 14.6 %copy-start = (bf16[256,1024]{1,0:T(8,128)(2,1)S(1)}, bf16[256,1024]{1,0:T(8,128)(2,1)}, u32[]{:S(2)}) copy-start(bf16[256,1024]{1,0:T(8,128)(2,1)} %param.26) | copy-start | bytes 1572868
  9.4 166.3 %copy-start.25 = (pred[256]{0:T(512)(128)(4,1)}, pred[256]{0:T(512)(128)(4,1)S(1)}, u32[]{:S(2)}) copy-start(pred[256]{0:T(512)(128)(4,1)S(1)} %get-tuple-element.124) | copy-start | bytes 772
  10.2 12.7 copy-start.15
  12.8 12.6 copy-start.22
  18.4 451.9 %copy-start.14 = (bf16[256,256]{0,1:T(8,128)(2,1)}, bf16[256,256]{0,1:T(8,128)(2,1)S(1)}, u32[]{:S(2)}) copy-start(bf16[256,256]{0,1:T(8,128)(2,1)S(1)} %fusion.44) | copy-start | bytes 393220
  21.7 446.7 %copy-start.21 = (f32[4,256]{1,0:T(4,128)}, f32[4,256]{1,0:T(4,128)S(1)}, u32[]{:S(2)}) copy-start(f32[4,256]{1,0:T(4,128)S(1)} %broadcast_add_fusion.4) | copy-start | bytes 12292
  22.9 60.4 %copy-start.2 = (bf16[256,1024]{1,0:T(8,128)(2,1)S(1)}, bf16[256,1024]{1,0:T(8,128)(2,1)}, u32[]{:S(2)}) copy-start(bf16[256,1024]{1,0:T(8,128)(2,1)} %param.18) | copy-start | bytes 1572868
  25.4 55.2 %all-to-all-start = ((f32[4,256,1024]{2,1,0:T(8,128)}), f32[4,256,1024]{2,1,0:T(8,128)}, u32[]{:S(2)}, u32[]{:S(2)}) async-start(f32[4,256,1024]{2,1,0:T(8,128)} %broadcast_in_dim.43), calls=%async_computation | async-start | bytes 8388608 | tf_op jit(solution)/shard_map/all_to_all | solution.py:17
  31.7 200.3 %copy-start.29 = (s32[256,1]{0,1:T(1,128)}, s32[256,1]{0,1:T(1,128)S(1)}, u32[]{:S(2)}) copy-start(s32[256,1]{0,1:T(1,128)S(1)} %get-tuple-element.145) | copy-start | bytes 3076
  95.0 54.6 %all-to-all-start.1 = ((f32[4,2,128,1024]{3,2,1,0:T(8,128)}), f32[4,2,128,1024]{3,2,1,0:T(8,128)}, u32[]{:S(2)}, u32[]{:S(2)}) async-start(f32[4,2,128,1024]{3,2,1,0:T(8,128)} %broadcast_in_dim.44), calls=%async_computation.1 | async-start | bytes 8388608 | tf_op jit(solution)/shard_map/all_to_all | solution.py:17
  169.1 54.6 %all-to-all-start.2 = ((f32[4,2,128,1024]{3,2,1,0:T(8,128)}), f32[4,2,128,1024]{3,2,1,0:T(8,128)}, u32[]{:S(2)}, u32[]{:S(2)}) async-start(f32[4,2,128,1024]{3,2,1,0:T(8,128)} %broadcast_in_dim.45), calls=%async_computation.2 | async-start | bytes 8388608 | tf_op jit(solution)/shard_map/all_to_all | solution.py:17
  174.8 128.7 %all-reduce.13.cloned.1.call-start = ((), (), s32[]{:S(2)}) async-start(), calls=%async_computation.8 | async-start | bytes 2097152 | tf_op jit(solution)/shard_map/psum | solution.py:213
  256.7 128.3 %all-reduce.15.cloned.1.call-start = ((), (), s32[]{:S(2)}) async-start(), calls=%async_computation.9 | async-start | bytes 2097152 | tf_op jit(solution)/shard_map/psum | solution.py:213
  320.1 201.3 %reduce-scatter.10.cloned.1.call-start = ((), (), s32[]{:S(2)}) async-start(), calls=%async_computation.11 | async-start | bytes 540672
  328.0 396.4 %reduce-scatter.12.cloned.1.call-start = ((), (), s32[]{:S(2)}) async-start(), calls=%async_computation.12 | async-start | bytes 540672
  335.9 542.4 %all-reduce.17.cloned.1.call-start = ((), (), s32[]{:S(2)}) async-start(), calls=%async_computation.13 | async-start | bytes 33554432
  373.4 969.9 %all-reduce.19.cloned.1.call-start = ((), (), s32[]{:S(2)}) async-start(), calls=%async_computation.14 | async-start | bytes 46137344
  432.0 31.4 %copy-start.30 = (s32[256,1]{0,1:T(1,128)S(1)}, s32[256,1]{0,1:T(1,128)}, u32[]{:S(2)}) copy-start(s32[256,1]{0,1:T(1,128)} %copy-done.29) | copy-start | bytes 3076
  485.7 25.9 %all-to-all-start.4 = ((f32[32,1,4613]{2,1,0:T(1,128)}), f32[32,1,4613]{2,1,0:T(1,128)}, u32[]{:S(2)}, u32[]{:S(2)}) async-start(f32[32,1,4613]{2,1,0:T(1,128)} %broadcast_in_dim.53), calls=%async_computation.4 | async-start | bytes 1212416 | tf_op jit(solution)/shard_map/all_to_all | solution.py:17
  492.9 27.2 %copy-start.34 = (u32[128]{0:T(128)S(1)}, u32[128]{0:T(128)}, u32[]{:S(2)}) copy-start(u32[128]{0:T(128)} %constant.61) | copy-start | bytes 1540
  494.9 230.9 %copy-start.13 = (bf16[4,64,256]{2,1,0:T(8,128)(2,1)S(1)}, bf16[4,64,256]{2,1,0:T(8,128)(2,1)}, u32[]{:S(2)}) copy-start(bf16[4,64,256]{2,1,0:T(8,128)(2,1)} %copy-done.12) | copy-start | bytes 393220
  514.0 220.9 %copy-start.23 = (f32[256]{0:T(256)S(1)}, f32[256]{0:T(256)}, u32[]{:S(2)}) copy-start(f32[256]{0:T(256)} %copy-done.22) | copy-start | bytes 3076
  514.0 217.7 %all-to-all-start.3 = ((f32[4,256,1024]{2,1,0:T(8,128)}), f32[4,256,1024]{2,1,0:T(8,128)}, u32[]{:S(2)}, u32[]{:S(2)}) async-start(f32[4,256,1024]{2,1,0:T(8,128)} %broadcast_in_dim.50), calls=%async_computation.3 | async-start | bytes 8388608 | tf_op jit(solution)/shard_map/all_to_all | solution.py:17
  519.9 830.3 %reduce-scatter.8.cloned.1.call-start = ((), (), s32[]{:S(2)}) async-start(), calls=%async_computation.10 | async-start | bytes 1081344 | tf_op jit(solution)/shard_map/reduce_scatter | solution.py:282
  (25 other events, 131.2 us)
Sparse Core Ops, SparseCore 0:
  256.8 46.7 all-reduce.12
  320.2 45.8 all-reduce.14
  373.5 452.8 all-reduce.16
  828.9 514.3 all-reduce.18
Sparse Core Ops, SparseCore 1:
  328.0 158.7 reduce-scatter.9
  489.1 235.2 reduce-scatter.11
  727.3 218.0 reduce-scatter.7
where the time goes:
time: 1370 us; the launch traced here: 1360 us
  waiting for transfers between devices  873 us (64%)
  local copies, waits for them, and re-layouts  147 us (11%)
  blocking collectives  140 us (10%)
  other arithmetic  81.3 us (6%)
  matrix products  66.8 us (5%)
  starting transfers between devices  31.9 us (2%)
  between operations  17.9 us (1%)
    unnamed x11, waiting for transfers between devices  665 us
    all_to_all x5, waiting for transfers between devices, copy_for_each(): lax.all_to_all(jnp.broadcast_to(x[None], (count, *x.shape)), axis, 0, 0,...  162 us
    unnamed x1, blocking collectives  140 us
    concatenate x2, local copies, waits for them, and re-layouts, in_one_piece(): jnp.concatenate([a.reshape(*a.shape[:along], w) for a, w in zip(arrays, w...  71.4 us
    psum x2, waiting for transfers between devices, local(): grad_normed_e = lax.psum(grad_normed_part, 'tensor')  46.4 us
    all_to_all x5, starting transfers between devices, copy_for_each(): lax.all_to_all(jnp.broadcast_to(x[None], (count, *x.shape)), axis, 0, 0,...  30.7 us
  transfers between devices with their start and end apart: 12, of which 7 were waited for; matrix products, arithmetic and copies ran while one was open for 14% of the time, Pallas kernels for 0%

commit v1 on v0

v1 whole, which is shorter than its diff:
```python
import math

import jax
import jax.numpy as jnp
from jax import lax
from jax.experimental import pallas as pl
from jax.experimental.pallas import tpu as pltpu
from jax.sharding import PartitionSpec as P

HD = 64
MESH = pl.DeviceIdType.MESH
VM = pltpu.VMEM
F32 = jnp.float32
BF = jnp.bfloat16
EPS = 1e-05
SCALE = HD ** (-0.5)
ROOT = math.sqrt(2.0 / math.pi)
COLS = [pl.ds(n * 256, 256) for n in range(4)]
LN_GAIN, LN_SHIFT, OUT_BIAS, CENT, GAIN, SHIFT, DOWN_B, UP_B, QV_B, STATS = (
    0, 1, 2, 3, 5, 9, 13, 17, 21, 22,
)


class Here:
    def __init__(self):
        d = lax.axis_index("dp")
        t = lax.axis_index("tensor")
        self.x, self.y, self.z = d // 16, (d // 4) % 4, d % 4
        self.h, self.c = t // 2, t % 2

    def dev(self, x=None, y=None, z=None, h=None, c=None):
        x = self.x if x is None else x
        y = self.y if y is None else y
        z = self.z if z is None else z
        h = self.h if h is None else h
        c = self.c if c is None else c
        return (x * 16 + y * 4 + z, h * 2 + c)

    def ring(self, axis, step, c=None):
        p = (getattr(self, axis) + step) % 4
        return self.dev(c=c, **{axis: p})


class Sems:
    def __init__(self, send, recv):
        self.send, self.recv, self.n = send, recv, 0

    def copy(self, src, dst, dev):
        k = self.n
        self.n += 1
        cp = pltpu.make_async_remote_copy(
            src_ref=src,
            dst_ref=dst,
            send_sem=self.send.at[k],
            recv_sem=self.recv.at[k],
            device_id=dev,
            device_id_type=MESH,
        )
        cp.start()
        return cp


def nn(a, b):
    return jnp.dot(a, b, preferred_element_type=F32)


def nt(a, b):
    return lax.dot_general(a, b, (((1,), (1,)), ((), ())), preferred_element_type=F32)


def tn(a, b):
    return lax.dot_general(a, b, (((0,), (0,)), ((), ())), preferred_element_type=F32)


def pick(hot, v):
    a = v.astype(BF)
    rest = v - a.astype(F32)
    b = rest.astype(BF)
    c = (rest - b.astype(F32)).astype(BF)
    return nn(hot, a) + nn(hot, b) + nn(hot, c)


def unit(v):
    center = v - jnp.mean(v, axis=-1, keepdims=True)
    r = lax.rsqrt(jnp.mean(center * center, axis=-1, keepdims=True) + EPS)
    return center * r, r


def unit_back(grad, gain, n, r):
    u = grad * gain
    return r * (u - jnp.mean(u, axis=-1, keepdims=True) - n * jnp.mean(u * n, axis=-1, keepdims=True))


def fold(v):
    return jnp.sum(v.reshape(v.shape[0] // 8, 8, v.shape[1]), axis=0)


def down_rows(v):
    return jnp.sum(v, axis=0, keepdims=True)


def rows32(i):
    return pl.ds(pl.multiple_of(i * 32, 32), 32)


class TensorSum:
    def __init__(self, here, sems, p, lc, lx, out):
        self.sems, self.p, self.lc, self.lx, self.out = sems, p, lc, lx, out
        self.core = here.dev(c=1 - here.c)
        self.across = here.dev(h=1 - here.h)
        self.mine = pl.ds(pl.multiple_of(here.c * 128, 128), 128)
        self.other = pl.ds(pl.multiple_of((1 - here.c) * 128, 128), 128)
        self.a, self.b, self.d = [], [], []

    def first(self, n):
        self.a.append(self.sems.copy(self.p.at[n, self.other], self.lc.at[n], self.core))

    def second(self, n):
        self.a[n].wait_recv()
        self.p[n, self.mine] = self.p[n, self.mine] + self.lc[n]
        self.b.append(self.sems.copy(self.p.at[n, self.mine], self.lx.at[n], self.across))

    def third(self, n):
        self.b[n].wait_recv()
        self.out[self.mine, COLS[n]] = self.p[n, self.mine] + self.lx[n]
        spot = self.out.at[self.mine, COLS[n]]
        self.d.append(self.sems.copy(spot, spot, self.core))

    def send(self, make):
        for n in range(4):
            self.p[n] = make(n)
            self.first(n)
            if n:
                self.second(n - 1)
        self.second(3)

    def end(self):
        for n in range(4):
            self.third(n)
        for cp in self.d:
            cp.wait_recv()
        for cp in self.a + self.b + self.d:
            cp.wait_send()


class RingSum:
    def __init__(self, here, axis, buf, base, rows, l1, l2, sems):
        self.p = getattr(here, axis)
        self.buf, self.base, self.rows = buf, base, rows
        self.l1, self.l2, self.sems = l1, l2, sems
        self.plus, self.minus = here.ring(axis, 1), here.ring(axis, 3)
        self.cps = []

    def part(self, step, half):
        n = self.rows // 2
        at = self.base + ((self.p + step) % 4) * self.rows + half * n
        return pl.ds(pl.multiple_of(at, n), n)

    def own(self):
        at = self.base + self.p * self.rows
        return pl.ds(pl.multiple_of(at, self.rows), self.rows)

    def start(self):
        n, buf, sems = self.rows // 2, self.buf, self.sems
        lo, hi = pl.ds(0, n), pl.ds(n, n)
        self.a = sems.copy(buf.at[self.part(2, 0)], self.l1.at[0], self.plus)
        self.b = sems.copy(buf.at[self.part(2, 1)], self.l1.at[1], self.minus)
        self.cps.append(sems.copy(buf.at[self.part(1, 1)], self.l2.at[0, hi], self.plus))
        self.cps.append(sems.copy(buf.at[self.part(3, 0)], self.l2.at[1, lo], self.minus))
        return self

    def middle(self):
        n, buf, sems = self.rows // 2, self.buf, self.sems
        lo, hi = pl.ds(0, n), pl.ds(n, n)
        up, dn = self.part(1, 0), self.part(3, 1)
        self.a.wait_recv()
        buf[up] = buf[up] + self.l1[0]
        self.cps.append(sems.copy(buf.at[up], self.l2.at[0, lo], self.plus))
        self.b.wait_recv()
        buf[dn] = buf[dn] + self.l1[1]
        self.cps.append(sems.copy(buf.at[dn], self.l2.at[1, hi], self.minus))

    def arrive(self):
        for cp in self.cps:
            cp.wait_recv()
        own = self.own()
        self.buf[own] = self.buf[own] + self.l2[0] + self.l2[1]

    def done(self):
        for cp in [self.a, self.b] + self.cps:
            cp.wait_send()


class Shared:
    def __init__(self, here, axis, buf, sems):
        self.here, self.axis, self.buf, self.sems = here, axis, buf, sems
        self.p = getattr(here, axis)

    def spot(self, step, half=None):
        at = ((self.p + step) % 4) * 256
        if half is None:
            return pl.ds(pl.multiple_of(at, 256), 256)
        return pl.ds(pl.multiple_of(at + half * 128, 128), 128)

    def start(self, src):
        rows = pl.ds(pl.multiple_of(self.here.c * 128, 128), 128)
        for half in range(2):
            self.buf[self.spot(0, half)] = src[rows, half * 512 : half * 512 + 512].astype(F32)
        mine = self.buf.at[self.spot(0)]
        self.near = [self.sems.copy(mine, mine, self.here.ring(self.axis, s)) for s in (1, 3)]
        return self

    def relay(self):
        self.far = []
        for cp, frm, to, half in ((self.near[0], 3, 1, 0), (self.near[1], 1, 3, 1)):
            cp.wait_recv()
            part = self.buf.at[self.spot(frm, half)]
            self.far.append(self.sems.copy(part, part, self.here.ring(self.axis, to)))

    def arrive(self):
        for cp in self.far:
            cp.wait_recv()

    def done(self):
        for cp in self.near + self.far:
            cp.wait_send()


class Moved:
    def __init__(self, here, axis, ys, gy, sems):
        self.here, self.axis, self.ys, self.gy, self.sems = here, axis, ys, gy, sems

    def start(self, src):
        here, axis, ys, gy = self.here, self.axis, self.ys, self.gy
        p, c = getattr(here, axis), here.c
        for q in range(4):
            ys[q] = src[:, q * 256 : q * 256 + 256].astype(F32)
        self.cps = []
        for step in (1, 3, 2, 0):
            for dc in range(2):
                q, e = (p + step) % 4, (c + dc) % 2
                rows = pl.ds(pl.multiple_of(e * 128, 128), 128)
                if step == 0 and dc == 0:
                    gy[p, c] = ys[q, rows]
                    continue
                to = here.ring(axis, step, c=e)
                self.cps.append(self.sems.copy(ys.at[q, rows], gy.at[p, c], to))
        return self

    def sent(self):
        for cp in self.cps:
            cp.wait_send()

    def arrive(self):
        for cp in self.cps:
            cp.wait_recv()


class ExpertGrads:
    def __init__(self, here, m, gs, gy, right, part, l1, l2, lx, land, sems):
        self.here, self.m, self.gs, self.gy, self.right = here, m, gs, gy, right
        self.part, self.lx, self.land, self.sems = part, lx, land, sems
        self.axis = ("y", "z")[m]
        self.ring = RingSum(here, ("z", "y")[m], part, 0, 256, l1, l2, sems)

    def multiply(self):
        for p in range(4):
            for k in range(2):
                self.right[p * 128 : p * 128 + 128, k * 256 : k * 256 + 256] = self.gy[p, k].astype(BF)

        def block(k, carry):
            lanes = pl.ds(pl.multiple_of((k % 4) * 128, 128), 128)
            left = [
                self.gs[pl.ds(pl.multiple_of(p * 256 + (k // 4) * 128, 128), 128), lanes].astype(BF)
                for p in range(4)
            ]
            res = tn(jnp.concatenate(left, axis=0), self.right[...])
            x, y = k // 4, k % 4
            if self.m == 0:
                for z in range(4):
                    at = pl.multiple_of(z * 256 + (x * 4 + y) * 32, 32)
                    self.part[pl.ds(at, 32)] = res[z * 32 : z * 32 + 32]
            else:
                self.part[pl.ds(pl.multiple_of(y * 256 + x * 128, 128), 128)] = res
            return carry

        lax.fori_loop(0, 8, block, 0)
        self.ring.start()

    def across(self):
        here, base = self.here, self.ring.p * 256
        self.ring.arrive()
        away = pl.ds(pl.multiple_of(base + (1 - here.x) * 128, 128), 128)
        self.swap = self.sems.copy(self.part.at[away], self.lx, here.dev(x=1 - here.x))

    def spread(self):
        here, base = self.here, self.ring.p * 256 + self.here.x * 128
        self.swap.wait_recv()
        mine = pl.ds(pl.multiple_of(base, 128), 128)
        self.part[mine] = self.part[mine] + self.lx[...]
        p, c = getattr(here, self.axis), here.c
        self.last = []
        for step in (1, 3, 2, 0):
            for dc in range(2):
                q, k = (p + step) % 4, (c + dc) % 2
                rows = pl.ds(pl.multiple_of(base + q * 32, 32), 32)
                lanes = pl.ds(pl.multiple_of(k * 256, 256), 256)
                if step == 0 and dc == 0:
                    self.land[p, c] = self.part[rows, lanes]
                    continue
                self.last.append(
                    self.sems.copy(
                        self.part.at[rows, lanes],
                        self.land.at[p, c],
                        here.ring(self.axis, step, c=k),
                    )
                )

    def finish(self, out, j):
        for cp in self.last:
            cp.wait_recv()
        for e in range(2):
            for q in range(4):
                out[e, j, :, q * 256 : q * 256 + 256] = self.land[q, e]
        for cp in [self.swap] + self.last:
            cp.wait_send()
        self.ring.done()


INPUTS = (
    "tok", "seg", "routes", "slots", "ln_gain", "ln_shift", "qkv_w", "qv_bias", "out_w", "out_bias",
    "cent", "ffn_gain", "ffn_shift", "up_w", "up_bias", "down_w", "down_bias", "cot",
)
IN_HBM = ("up_w", "down_w", "qkv_w", "out_w")
OUTPUTS = {
    "result": ((256, 1024), BF),
    "tokens_grad": ((256, 1024), BF),
    "qkv_grad": ((3, 32, 256), F32),
    "out_grad": ((32, 256), F32),
    "up_grad": ((2, 2, 32, 1024), F32),
    "down_grad": ((2, 2, 32, 1024), F32),
    "sums": ((24, 1024), F32),
}
PART = ((1024, 512), F32)
SQUARE = ((256, 1024), F32)
LOW = ((256, 1024), BF)
SCRATCH = {
    "wqkv": ((3, 1024, 256), BF), "wout": ((256, 1024), BF),
    "wup": ((2, 1024, 1024), BF), "wdn": ((2, 1024, 1024), BF),
    "normed": LOW, "q": ((256, 256), BF), "k": ((256, 256), BF), "v": ((256, 256), BF),
    "mixed": ((256, 256), BF), "probs": ((4, 256, 256), F32),
    "gq": ((256, 256), BF), "gk": ((256, 256), BF), "gv": ((256, 256), BF),
    "hot_s": ((256, 256), BF), "hot_t": ((256, 256), BF),
    "valid": ((256, 1), F32), "filled": ((256, 1), F32), "route": ((256, 1), F32),
    "sig": ((256, 1), F32), "gating": ((256, 1), F32), "segc": ((256, 1), F32),
    "hidden": SQUARE, "rows0": SQUARE, "rows1": SQUARE, "rows2": SQUARE,
    "slope0": SQUARE, "gwork": SQUARE, "grows": SQUARE, "ghidden": SQUARE,
    "n": LOW, "act": LOW, "go": LOW, "gp": LOW,
    "pa": ((4, 256, 256), F32), "lca": ((4, 128, 256), F32), "lxa": ((2, 4, 128, 256), F32),
    "pb": ((4, 256, 256), F32), "lcb": ((4, 128, 256), F32), "lxb": ((4, 128, 256), F32),
    "gs0u": PART, "gs0w": PART, "gs1u": PART, "gs1w": PART,
    "ysu": ((4, 256, 256), F32), "ysw": ((4, 256, 256), F32),
    "gy0u": ((4, 2, 128, 256), F32), "gy0w": ((4, 2, 128, 256), F32),
    "gy1u": ((4, 2, 128, 256), F32), "gy1w": ((4, 2, 128, 256), F32),
    "right": ((512, 512), BF),
    "partu": PART, "partw": PART,
    "l1": ((2, 2, 128, 512), F32), "l2": ((2, 2, 256, 512), F32),
    "lx": ((2, 2, 128, 512), F32), "land": ((2, 2, 4, 2, 32, 256), F32),
    "a1": ((2, 2, 128, 512), F32), "a2": ((2, 2, 256, 512), F32),
    "b1": ((2, 2, 32, 512), F32), "b2": ((2, 2, 64, 512), F32), "ax": ((2, 32, 512), F32),
    "vb": ((6, 24, 1024), F32), "lv": ((5, 24, 1024), F32),
}
N_SEMS = 240


class Bag:
    pass


def layer_kernel(*refs):
    B = Bag()
    for name, ref in zip([*INPUTS, *OUTPUTS, *SCRATCH, "ss", "rs", "ws"], refs):
        setattr(B, name, ref)
    B.n0 = B.n1 = B.gbranch = B.n
    B.act0 = B.act1 = B.act
    B.go0 = B.go1 = B.go
    B.gp0 = B.gp1 = B.gp
    here = Here()
    sems = Sems(B.ss, B.rs)
    x, c = here.x, here.c
    vec = B.vb.at[0]

    hops = [
        here.dev(y=here.y + 1 - 2 * (here.y % 2)),
        here.dev(y=3 - here.y),
        here.dev(z=here.z + 1 - 2 * (here.z % 2)),
        here.dev(z=3 - here.z),
        here.dev(x=1 - x),
    ]
    peers = [here.dev(c=1 - c), here.dev(h=1 - here.h), here.dev(x=1 - x)]
    for axis in ("y", "z"):
        for step in (1, 2, 3):
            for dc in range(2):
                peers.append(here.ring(axis, step, c=(c + dc) % 2))
    bar = pltpu.get_barrier_semaphore()
    for dev in peers:
        pl.semaphore_signal(bar, inc=1, device_id=dev, device_id_type=MESH)

    def fetch(pairs, at):
        cps = [pltpu.make_async_copy(s, t, B.ws.at[at + k]) for k, (s, t) in enumerate(pairs)]
        for cp in cps:
            cp.start()
        return cps

    def fetch_experts(j):
        return fetch(
            [(B.up_w.at[e, j], B.wup.at[e]) for e in range(2)]
            + [(B.down_w.at[e, j], B.wdn.at[e]) for e in range(2)],
            2,
        )

    heads = fetch([(B.qkv_w, B.wqkv), (B.out_w, B.wout)], 0)
    experts = fetch_experts(0)

    B.vb[0] = jnp.zeros((24, 1024), F32)
    lane1024 = lax.broadcasted_iota(jnp.int32, (1, 1024), 1)

    def stat(k, total):
        row = jnp.where(lane1024 == k, total, 0.0)
        vec[STATS : STATS + 1] = vec[STATS : STATS + 1] + row

    def total(v):
        return jnp.sum(jnp.sum(v, axis=1, keepdims=True), axis=0, keepdims=True)

    down_i = lax.broadcasted_iota(jnp.int32, (256, 256), 0)
    along_i = lax.broadcasted_iota(jnp.int32, (256, 256), 1)

    def column(row):
        return jnp.sum(jnp.where(down_i == along_i, row, 0.0), axis=1, keepdims=True)

    seg_row = B.seg[...].astype(F32)
    slot_row = jnp.concatenate([B.slots[0, 0:1], B.slots[0, 1:2]], axis=1)
    slot_col = column(slot_row.astype(F32))
    B.segc[...] = column(seg_row)
    B.route[...] = column(B.routes[...].astype(F32))
    B.valid[...] = (B.segc[...] != 0.0).astype(F32)
    B.filled[...] = (slot_col < 256.0).astype(F32)
    B.hot_s[...] = jnp.where(slot_col == along_i.astype(F32), 1.0, 0.0).astype(BF)
    B.hot_t[...] = jnp.where(slot_row == down_i, 1.0, 0.0).astype(BF)
    stat(4, total(B.valid[...]))

    def allowed():
        return (B.segc[...] == seg_row) & (along_i <= down_i) & (B.segc[...] != 0.0)

    head_of = along_i // HD

    gain = B.ln_gain[...].astype(F32)
    shift = B.ln_shift[...].astype(F32)

    def norm_block(i, carry):
        n, _ = unit(B.tok[rows32(i)].astype(F32))
        B.normed[rows32(i)] = (n * gain + shift).astype(BF)
        return carry

    lax.fori_loop(0, 8, norm_block, 0)
    for cp in heads:
        cp.wait()
    qv_bias = B.qv_bias[...].astype(F32)
    B.q[...] = (nn(B.normed[...], B.wqkv[0]) + qv_bias[0:1]).astype(BF)
    B.k[...] = nn(B.normed[...], B.wqkv[1]).astype(BF)
    B.v[...] = (nn(B.normed[...], B.wqkv[2]) + qv_bias[1:2]).astype(BF)

    def one_head(value, hh):
        return jnp.where(head_of == hh, value.astype(F32), 0.0)

    mixed = jnp.zeros((256, 256), F32)
    for hh in range(4):
        s = nt(one_head(B.q[...], hh).astype(BF), B.k[...]) * SCALE
        ok = allowed()
        s = jnp.where(ok, s, -1e30)
        e = jnp.where(ok, jnp.exp(s - jnp.max(s, axis=-1, keepdims=True)), 0.0)
        probs = e / (jnp.sum(e, axis=-1, keepdims=True) + (1.0 - B.valid[...]))
        B.probs[hh] = probs
        mixed = mixed + one_head(nn(probs.astype(BF), B.v[...]), hh)
    B.mixed[...] = mixed.astype(BF)

    pl.semaphore_wait(bar, len(peers))
    branch = TensorSum(here, sems, B.pa, B.lca, B.lxa.at[0], B.hidden)
    branch.send(lambda n: nn(B.mixed[...], B.wout[:, COLS[n]]))
    branch.end()

    out_bias = B.out_bias[...].astype(F32)
    cent = B.cent[...].astype(F32)

    def hidden_block(i, carry):
        rows = rows32(i)
        h = B.tok[rows].astype(F32) + (B.hidden[rows] + out_bias)
        B.hidden[rows] = h
        scores = [jnp.sum(h * cent[e : e + 1], axis=-1, keepdims=True) for e in range(2)]
        logits = jnp.where(B.route[rows] == 1.0, scores[1], scores[0])
        sig = 1.0 / (1.0 + jnp.exp(-logits))
        B.sig[rows] = sig
        B.gating[rows] = sig * B.valid[rows]
        return carry + fold(h * h * B.valid[rows])

    stat(0, total(lax.fori_loop(0, 8, hidden_block, jnp.zeros((8, 1024), F32))))
    for n in range(4):
        B.rows0[:, COLS[n]] = pick(B.hot_s[...], B.hidden[:, COLS[n]])
    ffn_gain = B.ffn_gain[...].astype(F32)
    ffn_shift = B.ffn_shift[...].astype(F32)
    up_bias = B.up_bias[...].astype(F32)
    down_bias = B.down_bias[...].astype(F32)

    def expert_norm(rows_ref, low_ref, j):
        for e in range(2):
            g, s = ffn_gain[e, j : j + 1], ffn_shift[e, j : j + 1]

            def block(i, carry, e=e, g=g, s=s):
                rows = rows32(e * 4 + i)
                n, _ = unit(rows_ref[rows])
                low_ref[rows] = (n * g + s).astype(BF)
                return carry

            lax.fori_loop(0, 4, block, 0)

    def gelu_parts(v):
        t = jnp.tanh(ROOT * (v + 0.044715 * (v * v * v)))
        cdf = 0.5 * (1.0 + t)
        slope = cdf + (0.5 * ROOT) * v * (1.0 - t * t) * (1.0 + (3.0 * 0.044715) * (v * v))
        return v * cdf, slope

    def half(e):
        return pl.ds(e * 128, 128)

    expert_norm(B.rows0, B.n0, 0)
    for cp in experts:
        cp.wait()
    for e in range(2):
        for n in range(4):
            pre = nn(B.n0[half(e)], B.wup[e, :, COLS[n]]) + up_bias[e, 0:1, n * 256 : n * 256 + 256]
            act, slope = gelu_parts(pre)
            B.act0[half(e), COLS[n]] = act.astype(BF)
            B.slope0[half(e), COLS[n]] = slope

    def down(act_ref):
        def make(n):
            return jnp.concatenate(
                [nn(act_ref[half(e)], B.wdn[e, :, COLS[n]]) for e in range(2)], axis=0
            )

        return make

    first = TensorSum(here, sems, B.pa, B.lca, B.lxa.at[1], B.rows1)
    first.send(down(B.act0))
    experts = fetch_experts(1)
    s0u = Shared(here, "y", B.gs0u, sems).start(B.n0)
    m0w = Moved(here, "z", B.ysw, B.gy0w, sems).start(B.act0)
    for n in range(4):
        g = pick(B.hot_s[...], B.gating[...] * B.cot[:, COLS[n]].astype(F32))
        B.grows[:, COLS[n]] = g
        B.go1[:, COLS[n]] = g.astype(BF)
    for e in range(2):
        vec[DOWN_B + e * 2 + 1 : DOWN_B + e * 2 + 2] = down_rows(B.go1[half(e)].astype(F32))
    s1w = Shared(here, "z", B.gs1w, sems).start(B.go1)
    for cp in experts:
        cp.wait()
    for e in range(2):
        for n in range(4):
            B.gwork[half(e), COLS[n]] = nt(B.go1[half(e)], B.wdn[e, COLS[n], :])
    first.end()

    sq = jnp.zeros((8, 1024), F32)
    for e in range(2):
        bias = down_bias[e, 0:1]

        def rows1_block(i, carry, e=e, bias=bias):
            rows = rows32(e * 4 + i)
            r1 = B.rows0[rows] + (B.rows1[rows] + bias)
            B.rows1[rows] = r1
            return carry + fold(r1 * r1 * B.filled[rows])

        sq = lax.fori_loop(0, 4, rows1_block, sq)
    stat(1, total(sq))
    expert_norm(B.rows1, B.n1, 1)
    for e in range(2):
        for n in range(4):
            pre = nn(B.n1[half(e)], B.wup[e, :, COLS[n]]) + up_bias[e, 1:2, n * 256 : n * 256 + 256]
            act, slope = gelu_parts(pre)
            B.act1[half(e), COLS[n]] = act.astype(BF)
            gp = (B.gwork[half(e), COLS[n]] * slope).astype(BF)
            B.gp1[half(e), COLS[n]] = gp
            vec[UP_B + e * 2 + 1 : UP_B + e * 2 + 2, COLS[n]] = down_rows(gp.astype(F32))

    def normed_grad(gp_ref):
        def make(n):
            return jnp.concatenate(
                [nt(gp_ref[half(e)], B.wup[e, COLS[n], :]) for e in range(2)], axis=0
            )

        return make

    back1 = TensorSum(here, sems, B.pa, B.lca, B.lxa.at[0], B.gwork)
    back1.send(normed_grad(B.gp1))
    m1u = Moved(here, "y", B.ysu, B.gy1u, sems).start(B.gp1)
    second = TensorSum(here, sems, B.pb, B.lcb, B.lxb, B.rows2)
    second.send(down(B.act1))
    experts = fetch_experts(0)
    s0u.relay()
    s1u = Shared(here, "y", B.gs1u, sems).start(B.n1)
    m0w.sent()
    m1w = Moved(here, "z", B.ysw, B.gy1w, sems).start(B.act1)
    s1w.relay()
    back1.end()

    def expert_norm_back(rows_ref, j, go_ref):
        for e in range(2):
            g = ffn_gain[e, j : j + 1]

            def block(i, carry, e=e, g=g):
                rows = rows32(e * 4 + i)
                n, r = unit(rows_ref[rows])
                gn = B.gwork[rows]
                new = B.grows[rows] + unit_back(gn, g, n, r)
                B.grows[rows] = new
                out = [carry[0] + fold(gn * n), carry[1] + fold(gn)]
                if go_ref is not None:
                    low = new.astype(BF)
                    go_ref[rows] = low
                    out.append(carry[2] + fold(low.astype(F32)))
                return tuple(out)

            zero = jnp.zeros((8, 1024), F32)
            sums = lax.fori_loop(0, 4, block, (zero,) * (2 if go_ref is None else 3))
            at = e * 2 + j
            vec[GAIN + at : GAIN + at + 1] = down_rows(sums[0])
            vec[SHIFT + at : SHIFT + at + 1] = down_rows(sums[1])
            if go_ref is not None:
                vec[DOWN_B + e * 2 : DOWN_B + e * 2 + 1] = down_rows(sums[2])

    expert_norm_back(B.rows1, 1, B.go0)
    for cp in experts:
        cp.wait()
    for e in range(2):
        for n in range(4):
            ga = nt(B.go0[half(e)], B.wdn[e, COLS[n], :])
            gp = (ga * B.slope0[half(e), COLS[n]]).astype(BF)
            B.gp0[half(e), COLS[n]] = gp
            vec[UP_B + e * 2 : UP_B + e * 2 + 1, COLS[n]] = down_rows(gp.astype(F32))
    back0 = TensorSum(here, sems, B.pa, B.lca, B.lxa.at[1], B.gwork)
    back0.send(normed_grad(B.gp0))
    s1u.relay()
    m1u.sent()
    m0u = Moved(here, "y", B.ysu, B.gy0u, sems).start(B.gp0)
    s0w = Shared(here, "z", B.gs0w, sems).start(B.go0)
    second.end()
    sq = jnp.zeros((8, 1024), F32)
    for e in range(2):
        bias = down_bias[e, 1:2]

        def rows2_block(i, carry, e=e, bias=bias):
            rows = rows32(e * 4 + i)
            r2 = B.rows1[rows] + (B.rows2[rows] + bias)
            B.rows2[rows] = r2
            return carry + fold(r2 * r2 * B.filled[rows])

        sq = lax.fori_loop(0, 4, rows2_block, sq)
    stat(2, total(sq))
    gate_grad = jnp.zeros((256, 1), F32)
    result_sq = jnp.zeros((256, 1), F32)
    for n in range(4):
        comb = pick(B.hot_t[...], B.rows2[:, COLS[n]])
        res = B.hidden[:, COLS[n]] + B.gating[...] * comb
        B.result[:, COLS[n]] = res.astype(BF)
        result_sq = result_sq + jnp.sum(res * res, axis=-1, keepdims=True)
        gate_grad = gate_grad + jnp.sum(B.cot[:, COLS[n]].astype(F32) * comb, axis=-1, keepdims=True)
    stat(3, total(result_sq * B.valid[...]))
    B.gating[...] = gate_grad * B.sig[...] * (1.0 - B.sig[...]) * B.valid[...]

    def gate_block(i, carry):
        rows = rows32(i)
        gl, second_route = B.gating[rows], B.route[rows] == 1.0
        B.ghidden[rows] = B.cot[rows].astype(F32) + gl * jnp.where(second_route, cent[1:2], cent[0:1])
        v = gl * B.hidden[rows]
        return (
            carry[0] + fold(jnp.where(second_route, 0.0, v)),
            carry[1] + fold(jnp.where(second_route, v, 0.0)),
        )

    zero = jnp.zeros((8, 1024), F32)
    sums = lax.fori_loop(0, 8, gate_block, (zero, zero))
    for e in range(2):
        vec[CENT + e : CENT + e + 1] = down_rows(sums[e])
    back0.end()

    expert_norm_back(B.rows0, 0, None)
    for n in range(4):
        g = B.ghidden[:, COLS[n]] + pick(B.hot_t[...], B.grows[:, COLS[n]])
        B.ghidden[:, COLS[n]] = g
        low = g.astype(BF)
        B.gbranch[:, COLS[n]] = low
        vec[OUT_BIAS : OUT_BIAS + 1, COLS[n]] = down_rows(low.astype(F32))
    gm = nt(B.gbranch[...], B.wout[...]).astype(BF)
    gq = jnp.zeros((256, 256), F32)
    gk = jnp.zeros((256, 256), F32)
    gv = jnp.zeros((256, 256), F32)
    for hh in range(4):
        probs = B.probs[hh]
        gp = nt(one_head(gm, hh).astype(BF), B.v[...])
        gv = gv + one_head(tn(probs.astype(BF), gm), hh)
        gs = (probs * (gp - jnp.sum(probs * gp, axis=-1, keepdims=True))).astype(BF)
        gq = gq + one_head(nn(gs, B.k[...]), hh)
        gk = gk + one_head(tn(gs, B.q[...]), hh)
    B.gq[...] = (gq * SCALE).astype(BF)
    B.gk[...] = (gk * SCALE).astype(BF)
    B.gv[...] = gv.astype(BF)
    vec[QV_B : QV_B + 1, 0:256] = down_rows(B.gq[...].astype(F32))
    vec[QV_B : QV_B + 1, 256:512] = down_rows(B.gv[...].astype(F32))
    back = TensorSum(here, sems, B.pa, B.lca, B.lxa.at[0], B.gwork)
    grads = (B.gq, B.gk, B.gv)
    back.send(lambda n: sum(nt(grads[s][...], B.wqkv[s, COLS[n], :]) for s in range(3)))

    s1u.arrive()
    s1w.arrive()
    m1u.arrive()
    m1w.arrive()
    eg1 = [
        ExpertGrads(here, m, (B.gs1u, B.gs1w)[m], (B.gy1u, B.gy1w)[m], B.right,
                    (B.partu, B.partw)[m], B.l1.at[m], B.l2.at[m], B.lx.at[0, m], B.land.at[0, m], sems)
        for m in range(2)
    ]
    for g in eg1:
        g.multiply()
    s0w.relay()
    s1u.done()
    s1w.done()
    lefts = (B.normed, B.normed, B.normed, B.gbranch)
    rights = (B.gq, B.gk, B.gv, B.mixed)
    apart = (B.gs1u, B.gs1w)
    rings = []
    for m in range(2):
        for j in range(2):

            def block(k, carry, m=m, left=lefts[2 * m + j], right=rights[2 * m + j], j=j):
                lanes = pl.ds(pl.multiple_of(k * 128, 128), 128)
                res = tn(left[:, lanes], right[...])
                for z in range(4):
                    if m == 0:
                        at = (k % 4) * 256 + (z * 2 + k // 4) * 32
                    else:
                        at = z * 256 + ((k % 4) * 2 + k // 4) * 32
                    apart[m][pl.ds(pl.multiple_of(at, 32), 32), j * 256 : j * 256 + 256] = res[
                        z * 32 : z * 32 + 32
                    ]
                return carry

            lax.fori_loop(0, 8, block, 0)
        rings.append(RingSum(here, ("y", "z")[m], apart[m], 0, 256, B.a1.at[m], B.a2.at[m], sems).start())
    back.end()

    zero = jnp.zeros((8, 1024), F32)

    def last_block(i, carry):
        rows = rows32(i)
        n, r = unit(B.tok[rows].astype(F32))
        gn = B.gwork[rows]
        B.tokens_grad[rows] = (B.ghidden[rows] + unit_back(gn, gain, n, r)).astype(BF)
        return carry[0] + fold(gn * n), carry[1] + fold(gn)

    sums = lax.fori_loop(0, 8, last_block, (zero, zero))
    vec[LN_GAIN : LN_GAIN + 1] = down_rows(sums[0])
    vec[LN_SHIFT : LN_SHIFT + 1] = down_rows(sums[1])
    hop_cps = []

    def hop(k):
        hop_cps.append(sems.copy(B.vb.at[k], B.lv.at[k], hops[k]))

    def hopped(k):
        hop_cps[k].wait_recv()
        B.vb[k + 1] = B.vb[k] + B.lv[k]

    hop(0)
    for g in eg1:
        g.ring.middle()
    for ring in rings:
        ring.middle()
    hopped(0)
    hop(1)
    for g in eg1:
        g.across()
    hopped(1)
    hop(2)
    for g in eg1:
        g.spread()
    s0u.arrive()
    s0w.arrive()
    m0u.arrive()
    m0w.arrive()
    for m, g in enumerate(eg1):
        g.finish((B.up_grad, B.down_grad)[m], 1)
    eg0 = [
        ExpertGrads(here, m, (B.gs0u, B.gs0w)[m], (B.gy0u, B.gy0w)[m], B.right,
                    (B.partu, B.partw)[m], B.l1.at[m], B.l2.at[m], B.lx.at[1, m], B.land.at[1, m], sems)
        for m in range(2)
    ]
    for g in eg0:
        g.multiply()
    hopped(2)
    hop(3)
    rings2 = []
    for m in range(2):
        rings[m].arrive()
        rings2.append(
            RingSum(here, ("z", "y")[m], apart[m], rings[m].p * 256, 64, B.b1.at[m], B.b2.at[m], sems).start()
        )
    for g in eg0:
        g.ring.middle()
    for ring in rings2:
        ring.middle()
    hopped(3)
    hop(4)
    swaps = []
    for m in range(2):
        rings2[m].arrive()
        base = rings2[m].base + rings2[m].p * 64
        away = pl.ds(pl.multiple_of(base + (1 - x) * 32, 32), 32)
        swaps.append(sems.copy(apart[m].at[away], B.ax.at[m], hops[4]))
    for g in eg0:
        g.across()
    for m in range(2):
        swaps[m].wait_recv()
        base = rings2[m].base + rings2[m].p * 64
        mine = apart[m][pl.ds(pl.multiple_of(base + x * 32, 32), 32)] + B.ax[m]
        if m == 0:
            B.qkv_grad[0] = mine[:, :256]
            B.qkv_grad[1] = mine[:, 256:]
        else:
            B.qkv_grad[2] = mine[:, :256]
            B.out_grad[...] = mine[:, 256:]
    for g in eg0:
        g.spread()
    hopped(4)
    B.sums[...] = B.vb[5]
    for m, g in enumerate(eg0):
        g.finish((B.up_grad, B.down_grad)[m], 0)
    for job in (m1u, m1w, m0u, m0w):
        if job in (m1w, m0u):
            job.sent()
    for job in (s0u, s0w, *rings, *rings2):
        job.done()
    for cp in hop_cps + swaps:
        cp.wait_send()


def local(
    tokens, segments, routes, slot_table, ln_gain, ln_shift, qkv_proj, qv_bias, out_proj, out_bias,
    centroids, ffn_gain, ffn_shift, up_proj, up_bias, down_proj, down_bias, cotangent,
):
    in_specs = [
        pl.BlockSpec(memory_space=pl.ANY if name in IN_HBM else VM) for name in INPUTS
    ]
    outs = pl.pallas_call(
        layer_kernel,
        out_shape=tuple(jax.ShapeDtypeStruct(*spec) for spec in OUTPUTS.values()),
        in_specs=in_specs,
        out_specs=[pl.BlockSpec(memory_space=VM)] * len(OUTPUTS),
        scratch_shapes=[VM(*spec) for spec in SCRATCH.values()]
        + [pltpu.SemaphoreType.DMA((N_SEMS,)), pltpu.SemaphoreType.DMA((N_SEMS,)), pltpu.SemaphoreType.DMA((6,))],
        compiler_params=pltpu.CompilerParams(
            collective_id=0, has_side_effects=True, vmem_limit_bytes=VMEM_LIMIT
        ),
    )(
        tokens, segments.reshape(1, 256), routes.reshape(1, 256), slot_table,
        ln_gain.reshape(1, 1024), ln_shift.reshape(1, 1024), qkv_proj, qv_bias, out_proj,
        out_bias.reshape(1, 1024), centroids, ffn_gain, ffn_shift, up_proj, up_bias, down_proj,
        down_bias, cotangent,
    )
    result, tokens_grad, qkv_grad, out_grad, up_grad, down_grad, sums = outs
    share = lax.dynamic_slice(sums[:17], (0, lax.axis_index("dp") * 32), (17, 32))
    totals = sums[STATS, :5]
    return (
        result,
        tokens_grad,
        share[LN_GAIN],
        share[LN_SHIFT],
        qkv_grad,
        sums[QV_B, :512].reshape(2, 256),
        out_grad.T,
        share[OUT_BIAS],
        share[CENT : CENT + 2],
        share[GAIN : GAIN + 4].reshape(2, 2, 32),
        share[SHIFT : SHIFT + 4].reshape(2, 2, 32),
        up_grad,
        sums[UP_B : UP_B + 4].reshape(2, 2, 1024),
        jnp.swapaxes(down_grad, 2, 3),
        share[DOWN_B : DOWN_B + 4].reshape(2, 2, 32),
        jnp.sqrt(totals[:4] / (totals[4] * 1024)),
    )


VMEM_LIMIT = 63 * 2**20


def solution(mesh):
    return jax.shard_map(
        local,
        mesh=mesh,
        in_specs=(
            P("dp", None),
            P("dp"),
            P("dp"),
            P("dp", None, None),
            P(),
            P(),
            P(None, None, "tensor"),
            P(None, "tensor"),
            P("tensor", None),
            P(),
            P(),
            P(),
            P(),
            P(None, None, None, "tensor"),
            P(None, None, "tensor"),
            P(None, None, "tensor", None),
            P(),
            P("dp", None),
        ),
        out_specs=(
            P("dp", None),
            P("dp", None),
            P("dp"),
            P("dp"),
            P(None, "dp", "tensor"),
            P(None, "tensor"),
            P("tensor", "dp"),
            P("dp"),
            P(None, "dp"),
            P(None, None, "dp"),
            P(None, None, "dp"),
            P(None, None, "dp", "tensor"),
            P(None, None, "tensor"),
            P(None, None, "tensor", "dp"),
            P(None, None, "dp"),
            P(),
        ),
        check_vma=False,
    )
```

time: 1370 us -> 234 us (0.17)
  waiting for transfers between devices: 873 us -> 0 us
  Pallas kernels: 0 us -> 209 us
  blocking collectives: 140 us -> 0 us
  local copies, waits for them, and re-layouts: 147 us -> 22.4 us
  other arithmetic: 81.3 us -> 1.2 us
  matrix products: 66.8 us -> 0 us
  starting transfers between devices: 31.9 us -> 0 us
  between operations: 17.9 us -> 1.32 us
    unnamed x11 -> x0, waiting for transfers between devices: 665 us -> none
    pallas_call x0 -> x1, Pallas kernels: none -> 209 us  [local(): pl.pallas_call(layer_kernel, out_shape=tuple((jax.ShapeDtypeStruct(*spec)...]
    all_to_all x5 -> x0, waiting for transfers between devices: 162 us -> none  [copy_for_each(): lax.all_to_all(jnp.broadcast_to(x[None], (count, *x.shape)), axis, 0, 0,...]
    unnamed x1 -> x0, blocking collectives: 140 us -> none
    concatenate x3 -> x0, local copies, waits for them, and re-layouts: 74.7 us -> none  [the longest x2 71.4 us: in_one_piece(): jnp.concatenate([a.reshape(*a.shape[:along], w) for a, w in zip(arrays, w...]
    dot_general x27 -> x0, matrix products: 63.4 us -> none  [the longest x2 11.8 us: local(): jnp.einsum('ecf,ecd->efd', act_low, grad_out_low, preferred_element_type=...]
    psum x2 -> x0, waiting for transfers between devices: 46.4 us -> none  [local(): grad_normed_e = lax.psum(grad_normed_part, 'tensor')]
    reduce_sum x23 -> x0, other arithmetic: 43 us -> none  [the longest x4 11.5 us: taken_together(): return jnp.sum(everything, axis=0)]
  transfers between devices with their start and end apart: 12 -> 0, of which waited for: 7 -> 0; matrix products, arithmetic and copies ran while one was open for 14% -> 0% of each run, Pallas kernels for 0% -> 0%
where the time goes in v1:
time: 234 us
  Pallas kernels  209 us (89%)
  local copies, waits for them, and re-layouts  22.4 us (10%)
    pallas_call x1, Pallas kernels, local(): pl.pallas_call(layer_kernel, out_shape=tuple((jax.ShapeDtypeStruct(*spec)...  209 us
    unnamed x6, local copies, waits for them, and re-layouts  10.4 us

profile of v1, /device:TPU:1, one launch (start us, length us, event | category | flops | bytes accessed | tf_op | source)
XLA Modules:
  0.0 233.6 jit_solution(17487896131418629391)
XLA Ops:
  0.6 1.3 reshape.69.refs_4_
  1.9 1.3 reshape.70.refs_5_
  3.2 1.3 reshape.71.refs_9_
  4.5 208.7 %shard_map.297 = (bf16[256,1024]{1,0:T(8,128)(2,1)}, bf16[256,1024]{1,0:T(8,128)(2,1)}, f32[3,32,256]{2,1,0:T(8,128)}, f32[32,256]{1,0:T(8,128)}, f32[2,2,32,102...) custom-call(bf16[256,1024]{1,0:T(8,128)(2,1)} %refs_0_.1, s32[1,256]{1,0:T(1,128)} %bitcast.25, ...), custom_call_target="tpu_custom_call" | custom-call | tf_op jit(solution)/shard_map/pallas_call | solution.py:861
  213.2 1.5 fusion
  214.7 1.4 dynamic-slice_bitcast_fusion
  216.0 1.3 slice.52
  217.9 1.2 sqrt_bitcast_fusion
  219.1 1.3 dynamic-slice.3
  220.4 0.8 slice.49
  221.2 0.6 reshape.74
  221.8 0.7 slice_reduce_fusion
  222.6 0.6 reshape_squeeze.3
  223.2 1.9 copy.40
  225.0 1.9 copy.41
  226.9 1.5 copy.42
  228.4 1.4 copy.43
  229.8 1.9 copy.44
  231.7 1.9 copy.45

commit v2 on v1

--- a/solution.py
+++ b/solution.py
@@ -135,7 +135,7 @@
         self.second(3)
 
     def end(self):
-        for n in range(4):
+        for n in range(len(self.d), 4):
             self.third(n)
         for cp in self.d:
             cp.wait_recv()
@@ -163,10 +163,10 @@
     def start(self):
         n, buf, sems = self.rows // 2, self.buf, self.sems
         lo, hi = pl.ds(0, n), pl.ds(n, n)
-        self.a = sems.copy(buf.at[self.part(2, 0)], self.l1.at[0], self.plus)
-        self.b = sems.copy(buf.at[self.part(2, 1)], self.l1.at[1], self.minus)
-        self.cps.append(sems.copy(buf.at[self.part(1, 1)], self.l2.at[0, hi], self.plus))
-        self.cps.append(sems.copy(buf.at[self.part(3, 0)], self.l2.at[1, lo], self.minus))
+        self.a = sems.copy(buf.at[self.part(2, 0)], self.l1[0], self.plus)
+        self.b = sems.copy(buf.at[self.part(2, 1)], self.l1[1], self.minus)
+        self.cps.append(sems.copy(buf.at[self.part(1, 1)], self.l2[0].at[hi], self.plus))
+        self.cps.append(sems.copy(buf.at[self.part(3, 0)], self.l2[1].at[lo], self.minus))
         return self
 
     def middle(self):
@@ -174,17 +174,17 @@
         lo, hi = pl.ds(0, n), pl.ds(n, n)
         up, dn = self.part(1, 0), self.part(3, 1)
         self.a.wait_recv()
-        buf[up] = buf[up] + self.l1[0]
-        self.cps.append(sems.copy(buf.at[up], self.l2.at[0, lo], self.plus))
+        buf[up] = buf[up] + self.l1[0][...]
+        self.cps.append(sems.copy(buf.at[up], self.l2[0].at[lo], self.plus))
         self.b.wait_recv()
-        buf[dn] = buf[dn] + self.l1[1]
-        self.cps.append(sems.copy(buf.at[dn], self.l2.at[1, hi], self.minus))
+        buf[dn] = buf[dn] + self.l1[1][...]
+        self.cps.append(sems.copy(buf.at[dn], self.l2[1].at[hi], self.minus))
 
     def arrive(self):
         for cp in self.cps:
             cp.wait_recv()
         own = self.own()
-        self.buf[own] = self.buf[own] + self.l2[0] + self.l2[1]
+        self.buf[own] = self.buf[own] + self.l2[0][...] + self.l2[1][...]
 
     def done(self):
         for cp in [self.a, self.b] + self.cps:
@@ -227,24 +227,26 @@
 
 
 class Moved:
-    def __init__(self, here, axis, ys, gy, sems):
+    def __init__(self, here, axis, lane, ys, gy, sems):
         self.here, self.axis, self.ys, self.gy, self.sems = here, axis, ys, gy, sems
+        self.lanes = pl.ds(lane, 256)
 
     def start(self, src):
-        here, axis, ys, gy = self.here, self.axis, self.ys, self.gy
+        here, axis, ys, gy, lanes = self.here, self.axis, self.ys, self.gy, self.lanes
         p, c = getattr(here, axis), here.c
         for q in range(4):
-            ys[q] = src[:, q * 256 : q * 256 + 256].astype(F32)
+            ys[q * 256 : q * 256 + 256, lanes] = src[:, q * 256 : q * 256 + 256].astype(F32)
+        spot = pl.ds(pl.multiple_of(p * 256 + c * 128, 128), 128)
         self.cps = []
         for step in (1, 3, 2, 0):
             for dc in range(2):
                 q, e = (p + step) % 4, (c + dc) % 2
-                rows = pl.ds(pl.multiple_of(e * 128, 128), 128)
+                rows = pl.ds(pl.multiple_of(q * 256 + e * 128, 128), 128)
                 if step == 0 and dc == 0:
-                    gy[p, c] = ys[q, rows]
+                    gy[spot, lanes] = ys[rows, lanes]
                     continue
                 to = here.ring(axis, step, c=e)
-                self.cps.append(self.sems.copy(ys.at[q, rows], gy.at[p, c], to))
+                self.cps.append(self.sems.copy(ys.at[rows, lanes], gy.at[spot, lanes], to))
         return self
 
     def sent(self):
@@ -257,21 +259,25 @@
 
 
 class ExpertGrads:
-    def __init__(self, here, m, gs, gy, right, part, l1, l2, lx, land, sems):
-        self.here, self.m, self.gs, self.gy, self.right = here, m, gs, gy, right
+    def __init__(self, here, m, shared, moved, right, part, l1, l2, lx, land, sems):
+        self.here, self.m, self.shared, self.moved, self.right = here, m, shared, moved, right
         self.part, self.lx, self.land, self.sems = part, lx, land, sems
         self.axis = ("y", "z")[m]
         self.ring = RingSum(here, ("z", "y")[m], part, 0, 256, l1, l2, sems)
 
     def multiply(self):
+        self.shared.arrive()
+        self.moved.arrive()
+        gs, gy, lanes = self.shared.buf, self.moved.gy, self.moved.lanes
         for p in range(4):
             for k in range(2):
-                self.right[p * 128 : p * 128 + 128, k * 256 : k * 256 + 256] = self.gy[p, k].astype(BF)
+                rows = pl.ds(p * 256 + k * 128, 128)
+                self.right[p * 128 : p * 128 + 128, k * 256 : k * 256 + 256] = gy[rows, lanes].astype(BF)
 
         def block(k, carry):
             lanes = pl.ds(pl.multiple_of((k % 4) * 128, 128), 128)
             left = [
-                self.gs[pl.ds(pl.multiple_of(p * 256 + (k // 4) * 128, 128), 128), lanes].astype(BF)
+                gs[pl.ds(pl.multiple_of(p * 256 + (k // 4) * 128, 128), 128), lanes].astype(BF)
                 for p in range(4)
             ]
             res = tn(jnp.concatenate(left, axis=0), self.right[...])
@@ -359,27 +365,65 @@
     "pa": ((4, 256, 256), F32), "lca": ((4, 128, 256), F32), "lxa": ((2, 4, 128, 256), F32),
     "pb": ((4, 256, 256), F32), "lcb": ((4, 128, 256), F32), "lxb": ((4, 128, 256), F32),
     "gs0u": PART, "gs0w": PART, "gs1u": PART, "gs1w": PART,
-    "ysu": ((4, 256, 256), F32), "ysw": ((4, 256, 256), F32),
-    "gy0u": ((4, 2, 128, 256), F32), "gy0w": ((4, 2, 128, 256), F32),
-    "gy1u": ((4, 2, 128, 256), F32), "gy1w": ((4, 2, 128, 256), F32),
+    "ys": PART, "gy0": PART, "gy1": PART,
     "right": ((512, 512), BF),
     "partu": PART, "partw": PART,
     "l1": ((2, 2, 128, 512), F32), "l2": ((2, 2, 256, 512), F32),
     "lx": ((2, 2, 128, 512), F32), "land": ((2, 2, 4, 2, 32, 256), F32),
     "a1": ((2, 2, 128, 512), F32), "a2": ((2, 2, 256, 512), F32),
     "b1": ((2, 2, 32, 512), F32), "b2": ((2, 2, 64, 512), F32), "ax": ((2, 32, 512), F32),
-    "vb": ((6, 24, 1024), F32), "lv": ((5, 24, 1024), F32),
+    "vb": ((10, 24, 1024), F32),
 }
 N_SEMS = 240
 
 
+class Totals:
+    def __init__(self, here, buf, sems):
+        self.here, self.buf, self.sems, self.cps = here, buf, sems, []
+        self.wait = []
+
+    def swap(self):
+        self.wait = [self.sems.copy(self.buf.at[0], self.buf.at[1], self.here.dev(x=1 - self.here.x))]
+        self.cps += self.wait
+
+    def collect(self):
+        for cp in self.wait:
+            cp.wait_recv()
+
+    def ring(self, axis):
+        buf, p = self.buf, getattr(self.here, axis)
+        at = (2 if axis == "y" else 6) + p
+        self.collect()
+        if axis == "y":
+            buf[at] = buf[0] + buf[1]
+        else:
+            buf[at] = (buf[2] + buf[3]) + (buf[4] + buf[5])
+        self.wait = [
+            self.sems.copy(buf.at[at], buf.at[at], self.here.ring(axis, step)) for step in (1, 3, 2)
+        ]
+        self.cps += self.wait
+
+    def finish(self, out):
+        self.collect()
+        buf = self.buf
+        out[...] = (buf[6] + buf[7]) + (buf[8] + buf[9])
+
+    def done(self):
+        for cp in self.cps:
+            cp.wait_send()
+
+
 class Bag:
     pass
 
 
+def two(ref):
+    return [ref.at[0], ref.at[1]]
+
+
 def layer_kernel(*refs):
     B = Bag()
-    for name, ref in zip([*INPUTS, *OUTPUTS, *SCRATCH, "ss", "rs", "ws"], refs):
+    for name, ref in zip([*INPUTS, *OUTPUTS, *SCRATCH, "ss", "rs", "ws", "free"], refs):
         setattr(B, name, ref)
     B.n0 = B.n1 = B.gbranch = B.n
     B.act0 = B.act1 = B.act
@@ -390,13 +434,6 @@
     x, c = here.x, here.c
     vec = B.vb.at[0]
 
-    hops = [
-        here.dev(y=here.y + 1 - 2 * (here.y % 2)),
-        here.dev(y=3 - here.y),
-        here.dev(z=here.z + 1 - 2 * (here.z % 2)),
-        here.dev(z=3 - here.z),
-        here.dev(x=1 - x),
-    ]
     peers = [here.dev(c=1 - c), here.dev(h=1 - here.h), here.dev(x=1 - x)]
     for axis in ("y", "z"):
         for step in (1, 2, 3):
@@ -454,8 +491,8 @@
 
     head_of = along_i // HD
 
-    gain = B.ln_gain[...].astype(F32)
-    shift = B.ln_shift[...].astype(F32)
+    gain = B.ln_gain[...].astype(F32).reshape(1, 1024)
+    shift = B.ln_shift[...].astype(F32).reshape(1, 1024)
 
     def norm_block(i, carry):
         n, _ = unit(B.tok[rows32(i)].astype(F32))
@@ -489,7 +526,7 @@
     branch.send(lambda n: nn(B.mixed[...], B.wout[:, COLS[n]]))
     branch.end()
 
-    out_bias = B.out_bias[...].astype(F32)
+    out_bias = B.out_bias[...].astype(F32).reshape(1, 1024)
     cent = B.cent[...].astype(F32)
 
     def hidden_block(i, carry):
@@ -554,7 +591,7 @@
     first.send(down(B.act0))
     experts = fetch_experts(1)
     s0u = Shared(here, "y", B.gs0u, sems).start(B.n0)
-    m0w = Moved(here, "z", B.ysw, B.gy0w, sems).start(B.act0)
+    m0w = Moved(here, "z", 256, B.ys, B.gy0, sems).start(B.act0)
     for n in range(4):
         g = pick(B.hot_s[...], B.gating[...] * B.cot[:, COLS[n]].astype(F32))
         B.grows[:, COLS[n]] = g
@@ -567,6 +604,9 @@
     for e in range(2):
         for n in range(4):
             B.gwork[half(e), COLS[n]] = nt(B.go1[half(e)], B.wdn[e, COLS[n], :])
+    for n in range(3):
+        first.third(n)
+    s0u.relay()
     first.end()
 
     sq = jnp.zeros((8, 1024), F32)
@@ -582,6 +622,7 @@
         sq = lax.fori_loop(0, 4, rows1_block, sq)
     stat(1, total(sq))
     expert_norm(B.rows1, B.n1, 1)
+    s1u = Shared(here, "y", B.gs1u, sems).start(B.n1)
     for e in range(2):
         for n in range(4):
             pre = nn(B.n1[half(e)], B.wup[e, :, COLS[n]]) + up_bias[e, 1:2, n * 256 : n * 256 + 256]
@@ -601,14 +642,12 @@
 
     back1 = TensorSum(here, sems, B.pa, B.lca, B.lxa.at[0], B.gwork)
     back1.send(normed_grad(B.gp1))
-    m1u = Moved(here, "y", B.ysu, B.gy1u, sems).start(B.gp1)
+    m1u = Moved(here, "y", 0, B.ys, B.gy1, sems).start(B.gp1)
     second = TensorSum(here, sems, B.pb, B.lcb, B.lxb, B.rows2)
     second.send(down(B.act1))
     experts = fetch_experts(0)
-    s0u.relay()
-    s1u = Shared(here, "y", B.gs1u, sems).start(B.n1)
     m0w.sent()
-    m1w = Moved(here, "z", B.ysw, B.gy1w, sems).start(B.act1)
+    m1w = Moved(here, "z", 256, B.ys, B.gy1, sems).start(B.act1)
     s1w.relay()
     back1.end()
 
@@ -638,6 +677,7 @@
                 vec[DOWN_B + e * 2 : DOWN_B + e * 2 + 1] = down_rows(sums[2])
 
     expert_norm_back(B.rows1, 1, B.go0)
+    s0w = Shared(here, "z", B.gs0w, sems).start(B.go0)
     for cp in experts:
         cp.wait()
     for e in range(2):
@@ -650,8 +690,13 @@
     back0.send(normed_grad(B.gp0))
     s1u.relay()
     m1u.sent()
-    m0u = Moved(here, "y", B.ysu, B.gy0u, sems).start(B.gp0)
-    s0w = Shared(here, "z", B.gs0w, sems).start(B.go0)
+    m0u = Moved(here, "y", 0, B.ys, B.gy0, sems).start(B.gp0)
+    eg1 = [
+        ExpertGrads(here, m, (s1u, s1w)[m], (m1u, m1w)[m], B.right, (B.partu, B.partw)[m],
+                    two(B.l1.at[m]), two(B.l2.at[m]), B.lx.at[0, m], B.land.at[0, m], sems)
+        for m in range(2)
+    ]
+    eg1[1].multiply()
     second.end()
     sq = jnp.zeros((8, 1024), F32)
     for e in range(2):
@@ -690,6 +735,14 @@
     sums = lax.fori_loop(0, 8, gate_block, (zero, zero))
     for e in range(2):
         vec[CENT + e : CENT + e + 1] = down_rows(sums[e])
+    for k, axis in enumerate(("z", "y")):
+        for step in (1, 3):
+            pl.semaphore_signal(
+                B.free.at[k], inc=1, device_id=here.ring(axis, step), device_id_type=MESH
+            )
+    for n in range(3):
+        back0.third(n)
+    s0w.relay()
     back0.end()
 
     expert_norm_back(B.rows0, 0, None)
@@ -719,18 +772,22 @@
     grads = (B.gq, B.gk, B.gv)
     back.send(lambda n: sum(nt(grads[s][...], B.wqkv[s, COLS[n], :]) for s in range(3)))
 
-    s1u.arrive()
-    s1w.arrive()
-    m1u.arrive()
-    m1w.arrive()
-    eg1 = [
-        ExpertGrads(here, m, (B.gs1u, B.gs1w)[m], (B.gy1u, B.gy1w)[m], B.right,
-                    (B.partu, B.partw)[m], B.l1.at[m], B.l2.at[m], B.lx.at[0, m], B.land.at[0, m], sems)
+    eg1[0].multiply()
+    m1w.sent()
+    m0u.sent()
+    wide = [pl.ds(0, 512), pl.ds(512, 512)]
+    eg0 = [
+        ExpertGrads(here, m, (s0u, s0w)[m], (m0u, m0w)[m], B.right, (B.ys, B.gy1)[m],
+                    [B.slope0.at[pl.ds(128 * k, 128), wide[m]] for k in range(2)],
+                    [(B.hidden, B.rows2)[m].at[:, wide[k]] for k in range(2)],
+                    B.lx.at[1, m], B.land.at[1, m], sems)
         for m in range(2)
     ]
-    for g in eg1:
-        g.multiply()
-    s0w.relay()
+    for m in range(2):
+        pl.semaphore_wait(B.free.at[m], 2)
+        eg0[m].multiply()
+    eg1[1].ring.middle()
+    eg1[0].ring.middle()
     s1u.done()
     s1w.done()
     lefts = (B.normed, B.normed, B.normed, B.gbranch)
@@ -754,7 +811,7 @@
                 return carry
 
             lax.fori_loop(0, 8, block, 0)
-        rings.append(RingSum(here, ("y", "z")[m], apart[m], 0, 256, B.a1.at[m], B.a2.at[m], sems).start())
+        rings.append(RingSum(here, ("y", "z")[m], apart[m], 0, 256, two(B.a1.at[m]), two(B.a2.at[m]), sems).start())
     back.end()
 
     zero = jnp.zeros((8, 1024), F32)
@@ -769,63 +826,42 @@
     sums = lax.fori_loop(0, 8, last_block, (zero, zero))
     vec[LN_GAIN : LN_GAIN + 1] = down_rows(sums[0])
     vec[LN_SHIFT : LN_SHIFT + 1] = down_rows(sums[1])
-    hop_cps = []
-
-    def hop(k):
-        hop_cps.append(sems.copy(B.vb.at[k], B.lv.at[k], hops[k]))
-
-    def hopped(k):
-        hop_cps[k].wait_recv()
-        B.vb[k + 1] = B.vb[k] + B.lv[k]
-
-    hop(0)
-    for g in eg1:
+    gather = Totals(here, B.vb, sems)
+    gather.swap()
+    eg1[1].across()
+    eg1[0].across()
+    for g in (eg0[1], eg0[0]):
         g.ring.middle()
     for ring in rings:
         ring.middle()
-    hopped(0)
-    hop(1)
-    for g in eg1:
-        g.across()
-    hopped(1)
-    hop(2)
+    gather.ring("y")
     for g in eg1:
         g.spread()
-    s0u.arrive()
-    s0w.arrive()
-    m0u.arrive()
-    m0w.arrive()
-    for m, g in enumerate(eg1):
-        g.finish((B.up_grad, B.down_grad)[m], 1)
-    eg0 = [
-        ExpertGrads(here, m, (B.gs0u, B.gs0w)[m], (B.gy0u, B.gy0w)[m], B.right,
-                    (B.partu, B.partw)[m], B.l1.at[m], B.l2.at[m], B.lx.at[1, m], B.land.at[1, m], sems)
-        for m in range(2)
-    ]
-    for g in eg0:
-        g.multiply()
-    hopped(2)
-    hop(3)
+    for g in (eg0[1], eg0[0]):
+        g.across()
+    gather.ring("z")
     rings2 = []
     for m in range(2):
         rings[m].arrive()
         rings2.append(
-            RingSum(here, ("z", "y")[m], apart[m], rings[m].p * 256, 64, B.b1.at[m], B.b2.at[m], sems).start()
+            RingSum(here, ("z", "y")[m], apart[m], rings[m].p * 256, 64,
+                    two(B.b1.at[m]), two(B.b2.at[m]), sems).start()
         )
-    for g in eg0:
-        g.ring.middle()
+    for g in (eg0[1], eg0[0]):
+        g.spread()
     for ring in rings2:
         ring.middle()
-    hopped(3)
-    hop(4)
+    for m, g in enumerate(eg1):
+        g.finish((B.up_grad, B.down_grad)[m], 1)
     swaps = []
     for m in range(2):
         rings2[m].arrive()
         base = rings2[m].base + rings2[m].p * 64
         away = pl.ds(pl.multiple_of(base + (1 - x) * 32, 32), 32)
-        swaps.append(sems.copy(apart[m].at[away], B.ax.at[m], hops[4]))
-    for g in eg0:
-        g.across()
+        swaps.append(sems.copy(apart[m].at[away], B.ax.at[m], here.dev(x=1 - x)))
+    gather.finish(B.sums)
+    for m, g in enumerate(eg0):
+        g.finish((B.up_grad, B.down_grad)[m], 0)
     for m in range(2):
         swaps[m].wait_recv()
         base = rings2[m].base + rings2[m].p * 64
@@ -836,19 +872,40 @@
         else:
             B.qkv_grad[2] = mine[:, :256]
             B.out_grad[...] = mine[:, 256:]
-    for g in eg0:
-        g.spread()
-    hopped(4)
-    B.sums[...] = B.vb[5]
-    for m, g in enumerate(eg0):
-        g.finish((B.up_grad, B.down_grad)[m], 0)
-    for job in (m1u, m1w, m0u, m0w):
-        if job in (m1w, m0u):
-            job.sent()
-    for job in (s0u, s0w, *rings, *rings2):
+    for job in (s0u, s0w, gather, *rings, *rings2):
         job.done()
-    for cp in hop_cps + swaps:
+    for cp in swaps:
         cp.wait_send()
+
+
+def finish_kernel(*refs):
+    big_in, sums, big_out = refs[:6], refs[6], refs[7:13]
+    gain, shift, out_b, cent, ffn_g, ffn_s, down_b, up_b, qv_b, rms, sem = refs[13:]
+    cps = [pltpu.make_async_copy(a, b, sem.at[k]) for k, (a, b) in enumerate(zip(big_in, big_out))]
+    for cp in cps:
+        cp.start()
+    d = lax.axis_index("dp")
+    near = sums[:, pl.ds(pl.multiple_of((d // 4) * 128, 128), 128)]
+    share = near[:, :32]
+    for k in range(1, 4):
+        share = jnp.where(d % 4 == k, near[:, k * 32 : k * 32 + 32], share)
+    for ref, at in ((gain, LN_GAIN), (shift, LN_SHIFT), (out_b, OUT_BIAS)):
+        ref[...] = share[at : at + 1]
+    cent[...] = share[CENT : CENT + 2]
+    for ref, at in ((ffn_g, GAIN), (ffn_s, SHIFT), (down_b, DOWN_B)):
+        for e in range(2):
+            ref[e] = share[at + e * 2 : at + e * 2 + 2]
+    for e in range(2):
+        up_b[e] = sums[UP_B + e * 2 : UP_B + e * 2 + 2]
+    qv_b[0:1] = sums[QV_B : QV_B + 1, 0:256]
+    qv_b[1:2] = sums[QV_B : QV_B + 1, 256:512]
+    totals = sums[STATS : STATS + 1, 0:128]
+    rms[...] = jnp.sqrt(totals[:, :4] / (totals[:, 4:5] * 1024.0))
+    for cp in cps:
+        cp.wait()
+
+
+SMALL = [(1, 32), (1, 32), (1, 32), (2, 32), (2, 2, 32), (2, 2, 32), (2, 2, 32), (2, 2, 1024), (2, 256), (1, 4)]
 
 
 def local(
@@ -864,36 +921,46 @@
         in_specs=in_specs,
         out_specs=[pl.BlockSpec(memory_space=VM)] * len(OUTPUTS),
         scratch_shapes=[VM(*spec) for spec in SCRATCH.values()]
-        + [pltpu.SemaphoreType.DMA((N_SEMS,)), pltpu.SemaphoreType.DMA((N_SEMS,)), pltpu.SemaphoreType.DMA((6,))],
+        + [pltpu.SemaphoreType.DMA((N_SEMS,)), pltpu.SemaphoreType.DMA((N_SEMS,)), pltpu.SemaphoreType.DMA((6,)), pltpu.SemaphoreType.REGULAR((2,))],
         compiler_params=pltpu.CompilerParams(
             collective_id=0, has_side_effects=True, vmem_limit_bytes=VMEM_LIMIT
         ),
     )(
         tokens, segments.reshape(1, 256), routes.reshape(1, 256), slot_table,
-        ln_gain.reshape(1, 1024), ln_shift.reshape(1, 1024), qkv_proj, qv_bias, out_proj,
-        out_bias.reshape(1, 1024), centroids, ffn_gain, ffn_shift, up_proj, up_bias, down_proj,
+        ln_gain, ln_shift, qkv_proj, qv_bias, out_proj,
+        out_bias, centroids, ffn_gain, ffn_shift, up_proj, up_bias, down_proj,
         down_bias, cotangent,
     )
-    result, tokens_grad, qkv_grad, out_grad, up_grad, down_grad, sums = outs
-    share = lax.dynamic_slice(sums[:17], (0, lax.axis_index("dp") * 32), (17, 32))
-    totals = sums[STATS, :5]
+    anywhere = pl.BlockSpec(memory_space=pl.ANY)
+    near = pl.BlockSpec(memory_space=VM)
+    (
+        result, tokens_grad, qkv_grad, out_grad, up_grad, down_grad,
+        gain, shift, out_b, cent, ffn_g, ffn_s, down_b, up_b, qv_b, rms,
+    ) = pl.pallas_call(
+        finish_kernel,
+        out_shape=tuple(jax.ShapeDtypeStruct(a.shape, a.dtype) for a in outs[:6])
+        + tuple(jax.ShapeDtypeStruct(shape, F32) for shape in SMALL),
+        in_specs=[near] * 7,
+        out_specs=[anywhere] * 6 + [near] * len(SMALL),
+        scratch_shapes=[pltpu.SemaphoreType.DMA((6,))],
+    )(*outs)
     return (
         result,
         tokens_grad,
-        share[LN_GAIN],
-        share[LN_SHIFT],
+        gain.reshape(32),
+        shift.reshape(32),
         qkv_grad,
-        sums[QV_B, :512].reshape(2, 256),
+        qv_b,
         out_grad.T,
-        share[OUT_BIAS],
-        share[CENT : CENT + 2],
-        share[GAIN : GAIN + 4].reshape(2, 2, 32),
-        share[SHIFT : SHIFT + 4].reshape(2, 2, 32),
+        out_b.reshape(32),
+        cent,
+        ffn_g,
+        ffn_s,
         up_grad,
-        sums[UP_B : UP_B + 4].reshape(2, 2, 1024),
+        up_b,
         jnp.swapaxes(down_grad, 2, 3),
-        share[DOWN_B : DOWN_B + 4].reshape(2, 2, 32),
-        jnp.sqrt(totals[:4] / (totals[4] * 1024)),
+        down_b,
+        rms.reshape(4),
     )
 
 

time: 234 us -> 184 us (0.79)
  Pallas kernels: 209 us -> 183 us
  local copies, waits for them, and re-layouts: 22.4 us -> 0 us
    pallas_call x1, Pallas kernels: 209 us -> 179 us  [local(): pl.pallas_call(layer_kernel, out_shape=tuple((jax.ShapeDtypeStruct(*spec)...]
    unnamed x6 -> x0, local copies, waits for them, and re-layouts: 10.4 us -> none
    slice x5 -> x0, local copies, waits for them, and re-layouts: 5.54 us -> none  [the longest x1 1.48 us: local(): share[DOWN_B:DOWN_B + 4].reshape(2, 2, 32)]
    reshape x4 -> x0, local copies, waits for them, and re-layouts: 4.46 us -> none  [the longest x1 1.28 us: local(): ln_gain.reshape(1, 1024)]
    pallas_call x0 -> x1, Pallas kernels: none -> 3.62 us  [local(): pl.pallas_call(finish_kernel, out_shape=tuple((jax.ShapeDtypeStruct(a.sha...]
where the time goes in v2:
time: 184 us
  Pallas kernels  183 us (99%)
    pallas_call x1, Pallas kernels, local(): pl.pallas_call(layer_kernel, out_shape=tuple((jax.ShapeDtypeStruct(*spec)...  179 us

profile of v2, /device:TPU:1, one launch (start us, length us, event | category | flops | bytes accessed | tf_op | source)
XLA Modules:
  0.0 183.9 jit_solution(8790474109851242160)
XLA Ops:
  0.7 179.4 %shard_map.297 = (bf16[256,1024]{1,0:T(8,128)(2,1)}, bf16[256,1024]{1,0:T(8,128)(2,1)}, f32[3,32,256]{2,1,0:T(8,128)}, f32[32,256]{1,0:T(8,128)}, f32[2,2,32,102...) custom-call(bf16[256,1024]{1,0:T(8,128)(2,1)} %refs_0_.1, s32[1,256]{1,0:T(1,128)} %bitcast.8, ...), custom_call_target="tpu_custom_call" | custom-call | tf_op jit(solution)/shard_map/pallas_call | solution.py:918
  180.1 3.6 %shard_map.298 = (bf16[256,1024]{1,0:T(8,128)(2,1)}, bf16[256,1024]{1,0:T(8,128)(2,1)}, f32[3,32,256]{2,1,0:T(8,128)}, f32[32,256]{1,0:T(8,128)}, f32[2,2,32,102...) custom-call(bf16[256,1024]{1,0:T(8,128)(2,1)} %get-tuple-element.39., ...), custom_call_target="tpu_custom_call" | custom-call | tf_op jit(solution)/shard_map/pallas_call | solution.py:939

commit v3 on v2

--- a/solution.py
+++ b/solution.py
@@ -9,6 +9,7 @@
 
 HD = 64
 MESH = pl.DeviceIdType.MESH
+OTHER = {"a": "b", "b": "a"}
 VM = pltpu.VMEM
 F32 = jnp.float32
 BF = jnp.bfloat16
@@ -27,6 +28,8 @@
         t = lax.axis_index("tensor")
         self.x, self.y, self.z = d // 16, (d // 4) % 4, d % 4
         self.h, self.c = t // 2, t % 2
+        self.a = self.y * (1 - self.c) + self.z * self.c
+        self.b = self.z * (1 - self.c) + self.y * self.c
 
     def dev(self, x=None, y=None, z=None, h=None, c=None):
         x = self.x if x is None else x
@@ -37,8 +40,9 @@
         return (x * 16 + y * 4 + z, h * 2 + c)
 
     def ring(self, axis, step, c=None):
-        p = (getattr(self, axis) + step) % 4
-        return self.dev(c=c, **{axis: p})
+        on_y = {"y": 1, "z": 0, "a": 1 - self.c, "b": self.c}[axis]
+        y, z = (self.y + step * on_y) % 4, (self.z + step * (1 - on_y)) % 4
+        return self.dev(y=y, z=z, c=c)
 
 
 class Sems:
@@ -205,7 +209,8 @@
     def start(self, src):
         rows = pl.ds(pl.multiple_of(self.here.c * 128, 128), 128)
         for half in range(2):
-            self.buf[self.spot(0, half)] = src[rows, half * 512 : half * 512 + 512].astype(F32)
+            part = src[rows, half * 512 : half * 512 + 512]
+            self.buf[self.spot(0, half)] = part.astype(F32)
         mine = self.buf.at[self.spot(0)]
         self.near = [self.sems.copy(mine, mine, self.here.ring(self.axis, s)) for s in (1, 3)]
         return self
@@ -232,15 +237,17 @@
         self.lanes = pl.ds(lane, 256)
 
     def start(self, src):
-        here, axis, ys, gy, lanes = self.here, self.axis, self.ys, self.gy, self.lanes
-        p, c = getattr(here, axis), here.c
+        here, ys, gy, lanes = self.here, self.ys, self.gy, self.lanes
+        c = here.c
         for q in range(4):
             ys[q * 256 : q * 256 + 256, lanes] = src[:, q * 256 : q * 256 + 256].astype(F32)
-        spot = pl.ds(pl.multiple_of(p * 256 + c * 128, 128), 128)
         self.cps = []
         for step in (1, 3, 2, 0):
             for dc in range(2):
-                q, e = (p + step) % 4, (c + dc) % 2
+                axis = self.axis if dc == 0 else OTHER[self.axis]
+                p, e = getattr(here, axis), (c + dc) % 2
+                q = (p + step) % 4
+                spot = pl.ds(pl.multiple_of(p * 256 + c * 128, 128), 128)
                 rows = pl.ds(pl.multiple_of(q * 256 + e * 128, 128), 128)
                 if step == 0 and dc == 0:
                     gy[spot, lanes] = ys[rows, lanes]
@@ -259,11 +266,11 @@
 
 
 class ExpertGrads:
-    def __init__(self, here, m, shared, moved, right, part, l1, l2, lx, land, sems):
+    def __init__(self, here, m, shared, moved, right, part, l1, l2, lx, land, sems, gates=None):
         self.here, self.m, self.shared, self.moved, self.right = here, m, shared, moved, right
-        self.part, self.lx, self.land, self.sems = part, lx, land, sems
-        self.axis = ("y", "z")[m]
-        self.ring = RingSum(here, ("z", "y")[m], part, 0, 256, l1, l2, sems)
+        self.part, self.lx, self.land, self.sems, self.gates = part, lx, land, sems, gates
+        self.axis = "ab"[m]
+        self.ring = RingSum(here, OTHER[self.axis], part, 0, 256, l1, l2, sems)
 
     def multiply(self):
         self.shared.arrive()
@@ -273,37 +280,43 @@
             for k in range(2):
                 rows = pl.ds(p * 256 + k * 128, 128)
                 self.right[p * 128 : p * 128 + 128, k * 256 : k * 256 + 256] = gy[rows, lanes].astype(BF)
+        gates = self.gates() if self.gates else None
+        ring_on_y = (self.m + self.here.c) % 2
+        per_y, per_z = 32 + 224 * ring_on_y, 256 - 224 * ring_on_y
 
         def block(k, carry):
             lanes = pl.ds(pl.multiple_of((k % 4) * 128, 128), 128)
-            left = [
-                gs[pl.ds(pl.multiple_of(p * 256 + (k // 4) * 128, 128), 128), lanes].astype(BF)
-                for p in range(4)
-            ]
+            left = []
+            for p in range(4):
+                v = gs[pl.ds(pl.multiple_of(p * 256 + (k // 4) * 128, 128), 128), lanes]
+                left.append((v if gates is None else gates[p] * v).astype(BF))
             res = tn(jnp.concatenate(left, axis=0), self.right[...])
-            x, y = k // 4, k % 4
-            if self.m == 0:
-                for z in range(4):
-                    at = pl.multiple_of(z * 256 + (x * 4 + y) * 32, 32)
-                    self.part[pl.ds(at, 32)] = res[z * 32 : z * 32 + 32]
-            else:
-                self.part[pl.ds(pl.multiple_of(y * 256 + x * 128, 128), 128)] = res
+            for z in range(4):
+                at = (k // 4) * 128 + (k % 4) * per_y + z * per_z
+                self.part[pl.ds(pl.multiple_of(at, 32), 32)] = res[z * 32 : z * 32 + 32]
             return carry
 
         lax.fori_loop(0, 8, block, 0)
         self.ring.start()
 
+    def send_x(self, base, rows):
+        here = self.here
+        away = pl.ds(pl.multiple_of(base + (1 - here.x) * rows, rows), rows)
+        self.swap = self.sems.copy(self.part.at[away], self.lx, here.dev(x=1 - here.x))
+
+    def add_x(self, base, rows):
+        self.swap.wait_recv()
+        mine = pl.ds(pl.multiple_of(base + self.here.x * rows, rows), rows)
+        self.part[mine] = self.part[mine] + self.lx[...]
+
     def across(self):
-        here, base = self.here, self.ring.p * 256
         self.ring.arrive()
-        away = pl.ds(pl.multiple_of(base + (1 - here.x) * 128, 128), 128)
-        self.swap = self.sems.copy(self.part.at[away], self.lx, here.dev(x=1 - here.x))
+        self.send_x(self.ring.p * 256, 128)
 
     def spread(self):
-        here, base = self.here, self.ring.p * 256 + self.here.x * 128
-        self.swap.wait_recv()
-        mine = pl.ds(pl.multiple_of(base, 128), 128)
-        self.part[mine] = self.part[mine] + self.lx[...]
+        here = self.here
+        self.add_x(self.ring.p * 256, 128)
+        base = self.ring.p * 256 + here.x * 128
         p, c = getattr(here, self.axis), here.c
         self.last = []
         for step in (1, 3, 2, 0):
@@ -369,48 +382,60 @@
     "right": ((512, 512), BF),
     "partu": PART, "partw": PART,
     "l1": ((2, 2, 128, 512), F32), "l2": ((2, 2, 256, 512), F32),
-    "lx": ((2, 2, 128, 512), F32), "land": ((2, 2, 4, 2, 32, 256), F32),
+    "lx": ((2, 2, 128, 512), F32), "gates": ((4, 8, 128), F32), "land": ((2, 2, 4, 2, 32, 256), F32),
     "a1": ((2, 2, 128, 512), F32), "a2": ((2, 2, 256, 512), F32),
     "b1": ((2, 2, 32, 512), F32), "b2": ((2, 2, 64, 512), F32), "ax": ((2, 32, 512), F32),
-    "vb": ((10, 24, 1024), F32),
+    "vb": ((11, 24, 1024), F32),
 }
 N_SEMS = 240
 
 
 class Totals:
     def __init__(self, here, buf, sems):
-        self.here, self.buf, self.sems, self.cps = here, buf, sems, []
-        self.wait = []
-
-    def swap(self):
-        self.wait = [self.sems.copy(self.buf.at[0], self.buf.at[1], self.here.dev(x=1 - self.here.x))]
+        self.here, self.buf, self.sems, self.cps, self.wait = here, buf, sems, [], []
+
+    def send(self, at, to, devices):
+        spots = self.buf.at[at], self.buf.at[to]
+        self.wait = [self.sems.copy(*spots, dev) for dev in devices]
         self.cps += self.wait
 
-    def collect(self):
+    def four(self, at):
         for cp in self.wait:
             cp.wait_recv()
-
-    def ring(self, axis):
-        buf, p = self.buf, getattr(self.here, axis)
-        at = (2 if axis == "y" else 6) + p
-        self.collect()
-        if axis == "y":
-            buf[at] = buf[0] + buf[1]
-        else:
-            buf[at] = (buf[2] + buf[3]) + (buf[4] + buf[5])
-        self.wait = [
-            self.sems.copy(buf.at[at], buf.at[at], self.here.ring(axis, step)) for step in (1, 3, 2)
-        ]
-        self.cps += self.wait
+        buf = self.buf
+        return (buf[at] + buf[at + 1]) + (buf[at + 2] + buf[at + 3])
+
+    def ring_y(self):
+        at = 1 + self.here.y
+        self.buf[at] = self.buf[0]
+        self.send(at, at, [self.here.ring("y", step) for step in (1, 3, 2)])
+
+    def ring_z(self):
+        at = 5 + self.here.z
+        self.buf[at] = self.four(1)
+        self.send(at, at, [self.here.ring("z", step) for step in (1, 3, 2)])
+
+    def pair(self):
+        self.buf[9] = self.four(5)
+        self.send(9, 10, [self.here.dev(x=1 - self.here.x)])
 
     def finish(self, out):
-        self.collect()
-        buf = self.buf
-        out[...] = (buf[6] + buf[7]) + (buf[8] + buf[9])
+        self.wait[0].wait_recv()
+        out[...] = self.buf[9] + self.buf[10]
 
     def done(self):
         for cp in self.cps:
             cp.wait_send()
+
+
+ORDER = (
+    "n1_relay", "gp0", "mul10", "back0_0", "go0_relay", "mul11", "rows2", "result", "mul00",
+    "back0_1", "mul01", "back0_2", "back0_end", "attention", "mid10", "mid00", "mid11", "x10",
+    "back_0", "mid01", "back_1", "attn1", "x01", "back_2", "tokens", "attn_mid1", "x11", "attn0",
+    "x00", "sums_z", "attn_mid0", "attn_next1", "spread01", "attn_next0", "attn_mid_next1",
+    "sums_x", "spread11", "attn_mid_next0", "spread00", "spread10", "sums_out", "attn_x1",
+    "attn_x0", "out00", "out01", "attn_out1", "out10", "out11", "attn_out0",
+)
 
 
 class Bag:
@@ -476,15 +501,8 @@
         return jnp.sum(jnp.where(down_i == along_i, row, 0.0), axis=1, keepdims=True)
 
     seg_row = B.seg[...].astype(F32)
-    slot_row = jnp.concatenate([B.slots[0, 0:1], B.slots[0, 1:2]], axis=1)
-    slot_col = column(slot_row.astype(F32))
     B.segc[...] = column(seg_row)
-    B.route[...] = column(B.routes[...].astype(F32))
     B.valid[...] = (B.segc[...] != 0.0).astype(F32)
-    B.filled[...] = (slot_col < 256.0).astype(F32)
-    B.hot_s[...] = jnp.where(slot_col == along_i.astype(F32), 1.0, 0.0).astype(BF)
-    B.hot_t[...] = jnp.where(slot_row == down_i, 1.0, 0.0).astype(BF)
-    stat(4, total(B.valid[...]))
 
     def allowed():
         return (B.segc[...] == seg_row) & (along_i <= down_i) & (B.segc[...] != 0.0)
@@ -524,6 +542,19 @@
     pl.semaphore_wait(bar, len(peers))
     branch = TensorSum(here, sems, B.pa, B.lca, B.lxa.at[0], B.hidden)
     branch.send(lambda n: nn(B.mixed[...], B.wout[:, COLS[n]]))
+    slot_row = jnp.concatenate([B.slots[0, 0:1], B.slots[0, 1:2]], axis=1)
+    slot_col = column(slot_row.astype(F32))
+    B.hot_s[...] = jnp.where(slot_col == along_i.astype(F32), 1.0, 0.0).astype(BF)
+    for n in range(4):
+        B.grows[:, COLS[n]] = nn(B.hot_s[...], B.cot[:, COLS[n]])
+    s1w = Shared(here, "b", B.gs1w, sems).start(B.grows)
+    B.route[...] = column(B.routes[...].astype(F32))
+    B.filled[...] = (slot_col < 256.0).astype(F32)
+    B.hot_t[...] = jnp.where(slot_row == down_i, 1.0, 0.0).astype(BF)
+    stat(4, total(B.valid[...]))
+    for n in range(2):
+        branch.third(n)
+    s1w.relay()
     branch.end()
 
     out_bias = B.out_bias[...].astype(F32).reshape(1, 1024)
@@ -570,6 +601,7 @@
         return pl.ds(e * 128, 128)
 
     expert_norm(B.rows0, B.n0, 0)
+    s0u = Shared(here, "a", B.gs0u, sems).start(B.n0)
     for cp in experts:
         cp.wait()
     for e in range(2):
@@ -590,15 +622,18 @@
     first = TensorSum(here, sems, B.pa, B.lca, B.lxa.at[1], B.rows1)
     first.send(down(B.act0))
     experts = fetch_experts(1)
-    s0u = Shared(here, "y", B.gs0u, sems).start(B.n0)
-    m0w = Moved(here, "z", 256, B.ys, B.gy0, sems).start(B.act0)
+    m0w = Moved(here, "b", 256, B.ys, B.gy0, sems).start(B.act0)
+    gate_row = down_rows(B.hot_t[...].astype(F32) * B.gating[...])
+    gate_col = column(gate_row)
+    B.gates[here.b] = jnp.broadcast_to(jnp.where(c == 0, gate_row[:, :128], gate_row[:, 128:]), (8, 128))
+    mine = B.gates.at[here.b]
+    gate_cps = [sems.copy(mine, mine, here.ring("b", step)) for step in (1, 3, 2)]
     for n in range(4):
-        g = pick(B.hot_s[...], B.gating[...] * B.cot[:, COLS[n]].astype(F32))
+        g = gate_col * B.grows[:, COLS[n]]
         B.grows[:, COLS[n]] = g
         B.go1[:, COLS[n]] = g.astype(BF)
     for e in range(2):
         vec[DOWN_B + e * 2 + 1 : DOWN_B + e * 2 + 2] = down_rows(B.go1[half(e)].astype(F32))
-    s1w = Shared(here, "z", B.gs1w, sems).start(B.go1)
     for cp in experts:
         cp.wait()
     for e in range(2):
@@ -622,7 +657,7 @@
         sq = lax.fori_loop(0, 4, rows1_block, sq)
     stat(1, total(sq))
     expert_norm(B.rows1, B.n1, 1)
-    s1u = Shared(here, "y", B.gs1u, sems).start(B.n1)
+    s1u = Shared(here, "a", B.gs1u, sems).start(B.n1)
     for e in range(2):
         for n in range(4):
             pre = nn(B.n1[half(e)], B.wup[e, :, COLS[n]]) + up_bias[e, 1:2, n * 256 : n * 256 + 256]
@@ -642,13 +677,12 @@
 
     back1 = TensorSum(here, sems, B.pa, B.lca, B.lxa.at[0], B.gwork)
     back1.send(normed_grad(B.gp1))
-    m1u = Moved(here, "y", 0, B.ys, B.gy1, sems).start(B.gp1)
+    m1u = Moved(here, "a", 0, B.ys, B.gy1, sems).start(B.gp1)
     second = TensorSum(here, sems, B.pb, B.lcb, B.lxb, B.rows2)
     second.send(down(B.act1))
     experts = fetch_experts(0)
     m0w.sent()
-    m1w = Moved(here, "z", 256, B.ys, B.gy1, sems).start(B.act1)
-    s1w.relay()
+    m1w = Moved(here, "b", 256, B.ys, B.gy1, sems).start(B.act1)
     back1.end()
 
     def expert_norm_back(rows_ref, j, go_ref):
@@ -677,7 +711,7 @@
                 vec[DOWN_B + e * 2 : DOWN_B + e * 2 + 1] = down_rows(sums[2])
 
     expert_norm_back(B.rows1, 1, B.go0)
-    s0w = Shared(here, "z", B.gs0w, sems).start(B.go0)
+    s0w = Shared(here, "b", B.gs0w, sems).start(B.go0)
     for cp in experts:
         cp.wait()
     for e in range(2):
@@ -688,93 +722,22 @@
             vec[UP_B + e * 2 : UP_B + e * 2 + 1, COLS[n]] = down_rows(gp.astype(F32))
     back0 = TensorSum(here, sems, B.pa, B.lca, B.lxa.at[1], B.gwork)
     back0.send(normed_grad(B.gp0))
-    s1u.relay()
-    m1u.sent()
-    m0u = Moved(here, "y", 0, B.ys, B.gy0, sems).start(B.gp0)
+    state = {}
+    def slot_gates():
+        for cp in gate_cps:
+            cp.wait_recv()
+        eye = down_i[:128, :128] == along_i[:128, :128]
+        return [
+            jnp.sum(jnp.where(eye, B.gates[p, 0:1], 0.0), axis=1, keepdims=True) for p in range(4)
+        ]
+
     eg1 = [
         ExpertGrads(here, m, (s1u, s1w)[m], (m1u, m1w)[m], B.right, (B.partu, B.partw)[m],
-                    two(B.l1.at[m]), two(B.l2.at[m]), B.lx.at[0, m], B.land.at[0, m], sems)
+                    two(B.l1.at[m]), two(B.l2.at[m]), B.lx.at[0, m], B.land.at[0, m], sems,
+                    gates=(None, slot_gates)[m])
         for m in range(2)
     ]
-    eg1[1].multiply()
-    second.end()
-    sq = jnp.zeros((8, 1024), F32)
-    for e in range(2):
-        bias = down_bias[e, 1:2]
-
-        def rows2_block(i, carry, e=e, bias=bias):
-            rows = rows32(e * 4 + i)
-            r2 = B.rows1[rows] + (B.rows2[rows] + bias)
-            B.rows2[rows] = r2
-            return carry + fold(r2 * r2 * B.filled[rows])
-
-        sq = lax.fori_loop(0, 4, rows2_block, sq)
-    stat(2, total(sq))
-    gate_grad = jnp.zeros((256, 1), F32)
-    result_sq = jnp.zeros((256, 1), F32)
-    for n in range(4):
-        comb = pick(B.hot_t[...], B.rows2[:, COLS[n]])
-        res = B.hidden[:, COLS[n]] + B.gating[...] * comb
-        B.result[:, COLS[n]] = res.astype(BF)
-        result_sq = result_sq + jnp.sum(res * res, axis=-1, keepdims=True)
-        gate_grad = gate_grad + jnp.sum(B.cot[:, COLS[n]].astype(F32) * comb, axis=-1, keepdims=True)
-    stat(3, total(result_sq * B.valid[...]))
-    B.gating[...] = gate_grad * B.sig[...] * (1.0 - B.sig[...]) * B.valid[...]
-
-    def gate_block(i, carry):
-        rows = rows32(i)
-        gl, second_route = B.gating[rows], B.route[rows] == 1.0
-        B.ghidden[rows] = B.cot[rows].astype(F32) + gl * jnp.where(second_route, cent[1:2], cent[0:1])
-        v = gl * B.hidden[rows]
-        return (
-            carry[0] + fold(jnp.where(second_route, 0.0, v)),
-            carry[1] + fold(jnp.where(second_route, v, 0.0)),
-        )
-
-    zero = jnp.zeros((8, 1024), F32)
-    sums = lax.fori_loop(0, 8, gate_block, (zero, zero))
-    for e in range(2):
-        vec[CENT + e : CENT + e + 1] = down_rows(sums[e])
-    for k, axis in enumerate(("z", "y")):
-        for step in (1, 3):
-            pl.semaphore_signal(
-                B.free.at[k], inc=1, device_id=here.ring(axis, step), device_id_type=MESH
-            )
-    for n in range(3):
-        back0.third(n)
-    s0w.relay()
-    back0.end()
-
-    expert_norm_back(B.rows0, 0, None)
-    for n in range(4):
-        g = B.ghidden[:, COLS[n]] + pick(B.hot_t[...], B.grows[:, COLS[n]])
-        B.ghidden[:, COLS[n]] = g
-        low = g.astype(BF)
-        B.gbranch[:, COLS[n]] = low
-        vec[OUT_BIAS : OUT_BIAS + 1, COLS[n]] = down_rows(low.astype(F32))
-    gm = nt(B.gbranch[...], B.wout[...]).astype(BF)
-    gq = jnp.zeros((256, 256), F32)
-    gk = jnp.zeros((256, 256), F32)
-    gv = jnp.zeros((256, 256), F32)
-    for hh in range(4):
-        probs = B.probs[hh]
-        gp = nt(one_head(gm, hh).astype(BF), B.v[...])
-        gv = gv + one_head(tn(probs.astype(BF), gm), hh)
-        gs = (probs * (gp - jnp.sum(probs * gp, axis=-1, keepdims=True))).astype(BF)
-        gq = gq + one_head(nn(gs, B.k[...]), hh)
-        gk = gk + one_head(tn(gs, B.q[...]), hh)
-    B.gq[...] = (gq * SCALE).astype(BF)
-    B.gk[...] = (gk * SCALE).astype(BF)
-    B.gv[...] = gv.astype(BF)
-    vec[QV_B : QV_B + 1, 0:256] = down_rows(B.gq[...].astype(F32))
-    vec[QV_B : QV_B + 1, 256:512] = down_rows(B.gv[...].astype(F32))
-    back = TensorSum(here, sems, B.pa, B.lca, B.lxa.at[0], B.gwork)
-    grads = (B.gq, B.gk, B.gv)
-    back.send(lambda n: sum(nt(grads[s][...], B.wqkv[s, COLS[n], :]) for s in range(3)))
-
-    eg1[0].multiply()
-    m1w.sent()
-    m0u.sent()
+    m0u = Moved(here, "a", 0, B.ys, B.gy0, sems)
     wide = [pl.ds(0, 512), pl.ds(512, 512)]
     eg0 = [
         ExpertGrads(here, m, (s0u, s0w)[m], (m0u, m0w)[m], B.right, (B.ys, B.gy1)[m],
@@ -783,86 +746,145 @@
                     B.lx.at[1, m], B.land.at[1, m], sems)
         for m in range(2)
     ]
-    for m in range(2):
-        pl.semaphore_wait(B.free.at[m], 2)
-        eg0[m].multiply()
-    eg1[1].ring.middle()
-    eg1[0].ring.middle()
-    s1u.done()
-    s1w.done()
     lefts = (B.normed, B.normed, B.normed, B.gbranch)
     rights = (B.gq, B.gk, B.gv, B.mixed)
     apart = (B.gs1u, B.gs1w)
-    rings = []
-    for m in range(2):
+    rings, rings2, swaps = {}, {}, {}
+    gather = Totals(here, B.vb, sems)
+
+    def move_gp0():
+        m1u.sent()
+        m0u.start(B.gp0)
+
+    def result():
+        sq = jnp.zeros((8, 1024), F32)
+        for e in range(2):
+            bias = down_bias[e, 1:2]
+
+            def rows2_block(i, carry, e=e, bias=bias):
+                rows = rows32(e * 4 + i)
+                r2 = B.rows1[rows] + (B.rows2[rows] + bias)
+                B.rows2[rows] = r2
+                return carry + fold(r2 * r2 * B.filled[rows])
+
+            sq = lax.fori_loop(0, 4, rows2_block, sq)
+        stat(2, total(sq))
+        gate_grad = jnp.zeros((256, 1), F32)
+        result_sq = jnp.zeros((256, 1), F32)
+        for n in range(4):
+            comb = pick(B.hot_t[...], B.rows2[:, COLS[n]])
+            res = B.hidden[:, COLS[n]] + B.gating[...] * comb
+            B.result[:, COLS[n]] = res.astype(BF)
+            result_sq = result_sq + jnp.sum(res * res, axis=-1, keepdims=True)
+            gate_grad = gate_grad + jnp.sum(B.cot[:, COLS[n]].astype(F32) * comb, axis=-1, keepdims=True)
+        stat(3, total(result_sq * B.valid[...]))
+        B.gating[...] = gate_grad * B.sig[...] * (1.0 - B.sig[...]) * B.valid[...]
+
+        def gate_block(i, carry):
+            rows = rows32(i)
+            gl, second_route = B.gating[rows], B.route[rows] == 1.0
+            B.ghidden[rows] = B.cot[rows].astype(F32) + gl * jnp.where(second_route, cent[1:2], cent[0:1])
+            v = gl * B.hidden[rows]
+            return (
+                carry[0] + fold(jnp.where(second_route, 0.0, v)),
+                carry[1] + fold(jnp.where(second_route, v, 0.0)),
+            )
+
+        zero = jnp.zeros((8, 1024), F32)
+        sums = lax.fori_loop(0, 8, gate_block, (zero, zero))
+        for e in range(2):
+            vec[CENT + e : CENT + e + 1] = down_rows(sums[e])
+        for k, axis in enumerate(("b", "a")):
+            for step in (1, 3):
+                pl.semaphore_signal(
+                    B.free.at[k], inc=1, device_id=here.ring(axis, step), device_id_type=MESH
+                )
+
+    def attention_back():
+        expert_norm_back(B.rows0, 0, None)
+        for n in range(4):
+            g = B.ghidden[:, COLS[n]] + pick(B.hot_t[...], B.grows[:, COLS[n]])
+            B.ghidden[:, COLS[n]] = g
+            low = g.astype(BF)
+            B.gbranch[:, COLS[n]] = low
+            vec[OUT_BIAS : OUT_BIAS + 1, COLS[n]] = down_rows(low.astype(F32))
+        gm = nt(B.gbranch[...], B.wout[...]).astype(BF)
+        gq = jnp.zeros((256, 256), F32)
+        gk = jnp.zeros((256, 256), F32)
+        gv = jnp.zeros((256, 256), F32)
+        for hh in range(4):
+            probs = B.probs[hh]
+            gp = nt(one_head(gm, hh).astype(BF), B.v[...])
+            gv = gv + one_head(tn(probs.astype(BF), gm), hh)
+            gs = (probs * (gp - jnp.sum(probs * gp, axis=-1, keepdims=True))).astype(BF)
+            gq = gq + one_head(nn(gs, B.k[...]), hh)
+            gk = gk + one_head(tn(gs, B.q[...]), hh)
+        B.gq[...] = (gq * SCALE).astype(BF)
+        B.gk[...] = (gk * SCALE).astype(BF)
+        B.gv[...] = gv.astype(BF)
+        vec[QV_B : QV_B + 1, 0:256] = down_rows(B.gq[...].astype(F32))
+        vec[QV_B : QV_B + 1, 256:512] = down_rows(B.gv[...].astype(F32))
+        state["back"] = back = TensorSum(here, sems, B.pa, B.lca, B.lxa.at[0], B.gwork)
+        grads = (B.gq, B.gk, B.gv)
+        back.send(lambda n: sum(nt(grads[s][...], B.wqkv[s, COLS[n], :]) for s in range(3)))
+
+
+    def first_sublayer(m):
+        if m == 0:
+            m1w.sent()
+            m0u.sent()
+        pl.semaphore_wait(B.free.at[m], 2)
+        eg0[m].multiply()
+
+    def attention_grads(m):
+        (s1u, s1w)[m].done()
+        last_y = (m + c) % 2
         for j in range(2):
 
-            def block(k, carry, m=m, left=lefts[2 * m + j], right=rights[2 * m + j], j=j):
+            def block(k, carry, m=m, last_y=last_y, left=lefts[2 * m + j], right=rights[2 * m + j], j=j):
                 lanes = pl.ds(pl.multiple_of(k * 128, 128), 128)
                 res = tn(left[:, lanes], right[...])
                 for z in range(4):
-                    if m == 0:
-                        at = (k % 4) * 256 + (z * 2 + k // 4) * 32
-                    else:
-                        at = z * 256 + ((k % 4) * 2 + k // 4) * 32
+                    at = (k // 4) * 32 + (k % 4) * (256 - 192 * last_y) + z * (64 + 192 * last_y)
                     apart[m][pl.ds(pl.multiple_of(at, 32), 32), j * 256 : j * 256 + 256] = res[
                         z * 32 : z * 32 + 32
                     ]
                 return carry
 
             lax.fori_loop(0, 8, block, 0)
-        rings.append(RingSum(here, ("y", "z")[m], apart[m], 0, 256, two(B.a1.at[m]), two(B.a2.at[m]), sems).start())
-    back.end()
-
-    zero = jnp.zeros((8, 1024), F32)
-
-    def last_block(i, carry):
-        rows = rows32(i)
-        n, r = unit(B.tok[rows].astype(F32))
-        gn = B.gwork[rows]
-        B.tokens_grad[rows] = (B.ghidden[rows] + unit_back(gn, gain, n, r)).astype(BF)
-        return carry[0] + fold(gn * n), carry[1] + fold(gn)
-
-    sums = lax.fori_loop(0, 8, last_block, (zero, zero))
-    vec[LN_GAIN : LN_GAIN + 1] = down_rows(sums[0])
-    vec[LN_SHIFT : LN_SHIFT + 1] = down_rows(sums[1])
-    gather = Totals(here, B.vb, sems)
-    gather.swap()
-    eg1[1].across()
-    eg1[0].across()
-    for g in (eg0[1], eg0[0]):
-        g.ring.middle()
-    for ring in rings:
-        ring.middle()
-    gather.ring("y")
-    for g in eg1:
-        g.spread()
-    for g in (eg0[1], eg0[0]):
-        g.across()
-    gather.ring("z")
-    rings2 = []
-    for m in range(2):
+        rings[m] = RingSum(here, "ab"[m], apart[m], 0, 256, two(B.a1.at[m]), two(B.a2.at[m]), sems)
+        rings[m].start()
+
+    def tokens_back():
+        state["back"].end()
+        zero = jnp.zeros((8, 1024), F32)
+
+        def last_block(i, carry):
+            rows = rows32(i)
+            n, r = unit(B.tok[rows].astype(F32))
+            gn = B.gwork[rows]
+            B.tokens_grad[rows] = (B.ghidden[rows] + unit_back(gn, gain, n, r)).astype(BF)
+            return carry[0] + fold(gn * n), carry[1] + fold(gn)
+
+        sums = lax.fori_loop(0, 8, last_block, (zero, zero))
+        vec[LN_GAIN : LN_GAIN + 1] = down_rows(sums[0])
+        vec[LN_SHIFT : LN_SHIFT + 1] = down_rows(sums[1])
+        gather.ring_y()
+
+    def second_ring(m):
         rings[m].arrive()
-        rings2.append(
-            RingSum(here, ("z", "y")[m], apart[m], rings[m].p * 256, 64,
-                    two(B.b1.at[m]), two(B.b2.at[m]), sems).start()
-        )
-    for g in (eg0[1], eg0[0]):
-        g.spread()
-    for ring in rings2:
-        ring.middle()
-    for m, g in enumerate(eg1):
-        g.finish((B.up_grad, B.down_grad)[m], 1)
-    swaps = []
-    for m in range(2):
+        base = rings[m].p * 256
+        b1, b2 = two(B.b1.at[m]), two(B.b2.at[m])
+        rings2[m] = RingSum(here, "ba"[m], apart[m], base, 64, b1, b2, sems)
+        rings2[m].start()
+
+    def attention_swap(m):
         rings2[m].arrive()
         base = rings2[m].base + rings2[m].p * 64
         away = pl.ds(pl.multiple_of(base + (1 - x) * 32, 32), 32)
-        swaps.append(sems.copy(apart[m].at[away], B.ax.at[m], here.dev(x=1 - x)))
-    gather.finish(B.sums)
-    for m, g in enumerate(eg0):
-        g.finish((B.up_grad, B.down_grad)[m], 0)
-    for m in range(2):
+        swaps[m] = sems.copy(apart[m].at[away], B.ax.at[m], here.dev(x=1 - x))
+
+    def attention_out(m):
         swaps[m].wait_recv()
         base = rings2[m].base + rings2[m].p * 64
         mine = apart[m][pl.ds(pl.multiple_of(base + x * 32, 32), 32)] + B.ax[m]
@@ -872,9 +894,42 @@
         else:
             B.qkv_grad[2] = mine[:, :256]
             B.out_grad[...] = mine[:, 256:]
-    for job in (s0u, s0w, gather, *rings, *rings2):
+
+    steps = {
+        "n1_relay": s1u.relay,
+        "gp0": move_gp0,
+        "rows2": second.end,
+        "result": result,
+        "go0_relay": s0w.relay,
+        "back0_end": back0.end,
+        "attention": attention_back,
+        "tokens": tokens_back,
+        "sums_z": gather.ring_z,
+        "sums_x": gather.pair,
+        "sums_out": lambda: gather.finish(B.sums),
+    }
+    for n in range(3):
+        steps[f"back0_{n}"] = lambda n=n: back0.third(n)
+        steps[f"back_{n}"] = lambda n=n: state["back"].third(n)
+    for m in range(2):
+        for j, g in ((1, eg1[m]), (0, eg0[m])):
+            at = f"{j}{m}"
+            steps["mul" + at] = g.multiply if j else lambda m=m: first_sublayer(m)
+            steps["mid" + at] = g.ring.middle
+            steps["x" + at] = g.across
+            steps["spread" + at] = g.spread
+            steps["out" + at] = lambda g=g, m=m, j=j: g.finish((B.up_grad, B.down_grad)[m], j)
+        steps[f"attn{m}"] = lambda m=m: attention_grads(m)
+        steps[f"attn_mid{m}"] = lambda m=m: rings[m].middle()
+        steps[f"attn_next{m}"] = lambda m=m: second_ring(m)
+        steps[f"attn_mid_next{m}"] = lambda m=m: rings2[m].middle()
+        steps[f"attn_x{m}"] = lambda m=m: attention_swap(m)
+        steps[f"attn_out{m}"] = lambda m=m: attention_out(m)
+    for name in ORDER:
+        steps[name]()
+    for job in (s0u, s0w, gather, *rings.values(), *rings2.values()):
         job.done()
-    for cp in swaps:
+    for cp in [*swaps.values(), *gate_cps]:
         cp.wait_send()
 
 

time: 184 us -> 178 us (0.967)
  Pallas kernels: 183 us -> 176 us
    pallas_call x1, Pallas kernels: 179 us -> 172 us  [local(): pl.pallas_call(layer_kernel, out_shape=tuple((jax.ShapeDtypeStruct(*spec)...]
where the time goes in v3:
time: 178 us; the launch traced here: 177 us
  Pallas kernels  176 us (99%)
    pallas_call x1, Pallas kernels, local(): pl.pallas_call(layer_kernel, out_shape=tuple((jax.ShapeDtypeStruct(*spec)...  172 us
    pallas_call x1, Pallas kernels, local(): pl.pallas_call(finish_kernel, out_shape=tuple((jax.ShapeDtypeStruct(a.sha...  3.62 us

profile of v3, /device:TPU:1, one launch (start us, length us, event | category | flops | bytes accessed | tf_op | source)
XLA Modules:
  0.0 176.7 jit_solution(8878382861356151558)
XLA Ops:
  0.7 172.3 %shard_map.297 = (bf16[256,1024]{1,0:T(8,128)(2,1)}, bf16[256,1024]{1,0:T(8,128)(2,1)}, f32[3,32,256]{2,1,0:T(8,128)}, f32[32,256]{1,0:T(8,128)}, f32[2,2,32,102...) custom-call(bf16[256,1024]{1,0:T(8,128)(2,1)} %refs_0_.1, s32[1,256]{1,0:T(1,128)} %bitcast.8, ...), custom_call_target="tpu_custom_call" | custom-call | tf_op jit(solution)/shard_map/pallas_call | solution.py:973
  172.9 3.6 %shard_map.298 = (bf16[256,1024]{1,0:T(8,128)(2,1)}, bf16[256,1024]{1,0:T(8,128)(2,1)}, f32[3,32,256]{2,1,0:T(8,128)}, f32[32,256]{1,0:T(8,128)}, f32[2,2,32,102...) custom-call(bf16[256,1024]{1,0:T(8,128)(2,1)} %get-tuple-element.39., ...), custom_call_target="tpu_custom_call" | custom-call | tf_op jit(solution)/shard_map/pallas_call | solution.py:994

commit v4 on v3

--- a/solution.py
+++ b/solution.py
@@ -49,9 +49,19 @@
     def __init__(self, send, recv):
         self.send, self.recv, self.n = send, recv, 0
 
-    def copy(self, src, dst, dev):
-        k = self.n
-        self.n += 1
+    def block(self, n):
+        self.n += n
+        return self.n - n
+
+    def all_recv(self, k, view):
+        pltpu.make_async_copy(view, view, self.recv.at[k]).wait()
+
+    def all_sent(self, k, view):
+        pltpu.make_async_copy(view, view, self.send.at[k]).wait()
+
+    def copy(self, src, dst, dev, k=None):
+        if k is None:
+            k = self.block(1)
         cp = pltpu.make_async_remote_copy(
             src_ref=src,
             dst_ref=dst,
@@ -108,8 +118,8 @@
 
 
 class TensorSum:
-    def __init__(self, here, sems, p, lc, lx, out):
-        self.sems, self.p, self.lc, self.lx, self.out = sems, p, lc, lx, out
+    def __init__(self, here, sems, p, lc, lx, out, at):
+        self.sems, self.p, self.lc, self.lx, self.out, self.at = sems, p, lc, lx, out, at
         self.core = here.dev(c=1 - here.c)
         self.across = here.dev(h=1 - here.h)
         self.mine = pl.ds(pl.multiple_of(here.c * 128, 128), 128)
@@ -117,18 +127,20 @@
         self.a, self.b, self.d = [], [], []
 
     def first(self, n):
-        self.a.append(self.sems.copy(self.p.at[n, self.other], self.lc.at[n], self.core))
+        cp = self.sems.copy(self.p.at[n, self.other], self.lc.at[n], self.core, self.at[0] + n)
+        self.a.append(cp)
 
     def second(self, n):
         self.a[n].wait_recv()
         self.p[n, self.mine] = self.p[n, self.mine] + self.lc[n]
-        self.b.append(self.sems.copy(self.p.at[n, self.mine], self.lx.at[n], self.across))
+        cp = self.sems.copy(self.p.at[n, self.mine], self.lx.at[n], self.across, self.at[1] + n)
+        self.b.append(cp)
 
     def third(self, n):
         self.b[n].wait_recv()
         self.out[self.mine, COLS[n]] = self.p[n, self.mine] + self.lx[n]
         spot = self.out.at[self.mine, COLS[n]]
-        self.d.append(self.sems.copy(spot, spot, self.core))
+        self.d.append(self.sems.copy(spot, spot, self.core, self.at[2] + n))
 
     def send(self, make):
         for n in range(4):
@@ -241,7 +253,7 @@
         c = here.c
         for q in range(4):
             ys[q * 256 : q * 256 + 256, lanes] = src[:, q * 256 : q * 256 + 256].astype(F32)
-        self.cps = []
+        self.k = self.sems.block(1)
         for step in (1, 3, 2, 0):
             for dc in range(2):
                 axis = self.axis if dc == 0 else OTHER[self.axis]
@@ -253,16 +265,14 @@
                     gy[spot, lanes] = ys[rows, lanes]
                     continue
                 to = here.ring(axis, step, c=e)
-                self.cps.append(self.sems.copy(ys.at[rows, lanes], gy.at[spot, lanes], to))
+                self.sems.copy(ys.at[rows, lanes], gy.at[spot, lanes], to, self.k)
         return self
 
     def sent(self):
-        for cp in self.cps:
-            cp.wait_send()
+        self.sems.all_sent(self.k, self.ys.at[pl.ds(0, 896), self.lanes])
 
     def arrive(self):
-        for cp in self.cps:
-            cp.wait_recv()
+        self.sems.all_recv(self.k, self.gy.at[pl.ds(0, 896), self.lanes])
 
 
 class ExpertGrads:
@@ -318,7 +328,7 @@
         self.add_x(self.ring.p * 256, 128)
         base = self.ring.p * 256 + here.x * 128
         p, c = getattr(here, self.axis), here.c
-        self.last = []
+        self.k = self.sems.block(1)
         for step in (1, 3, 2, 0):
             for dc in range(2):
                 q, k = (p + step) % 4, (c + dc) % 2
@@ -327,22 +337,17 @@
                 if step == 0 and dc == 0:
                     self.land[p, c] = self.part[rows, lanes]
                     continue
-                self.last.append(
-                    self.sems.copy(
-                        self.part.at[rows, lanes],
-                        self.land.at[p, c],
-                        here.ring(self.axis, step, c=k),
-                    )
-                )
+                to = here.ring(self.axis, step, c=k)
+                self.sems.copy(self.part.at[rows, lanes], self.land.at[p, c], to, self.k)
 
     def finish(self, out, j):
-        for cp in self.last:
-            cp.wait_recv()
+        seven = self.part.at[pl.ds(0, 224), pl.ds(0, 256)]
+        self.sems.all_recv(self.k, seven)
         for e in range(2):
             for q in range(4):
                 out[e, j, :, q * 256 : q * 256 + 256] = self.land[q, e]
-        for cp in [self.swap] + self.last:
-            cp.wait_send()
+        self.sems.all_sent(self.k, seven)
+        self.swap.wait_send()
         self.ring.done()
 
 
@@ -387,7 +392,7 @@
     "b1": ((2, 2, 32, 512), F32), "b2": ((2, 2, 64, 512), F32), "ax": ((2, 32, 512), F32),
     "vb": ((11, 24, 1024), F32),
 }
-N_SEMS = 240
+N_SEMS = 116
 
 
 class Totals:
@@ -426,16 +431,6 @@
     def done(self):
         for cp in self.cps:
             cp.wait_send()
-
-
-ORDER = (
-    "n1_relay", "gp0", "mul10", "back0_0", "go0_relay", "mul11", "rows2", "result", "mul00",
-    "back0_1", "mul01", "back0_2", "back0_end", "attention", "mid10", "mid00", "mid11", "x10",
-    "back_0", "mid01", "back_1", "attn1", "x01", "back_2", "tokens", "attn_mid1", "x11", "attn0",
-    "x00", "sums_z", "attn_mid0", "attn_next1", "spread01", "attn_next0", "attn_mid_next1",
-    "sums_x", "spread11", "attn_mid_next0", "spread00", "spread10", "sums_out", "attn_x1",
-    "attn_x0", "out00", "out01", "attn_out1", "out10", "out11", "attn_out0",
-)
 
 
 class Bag:
@@ -458,6 +453,8 @@
     sems = Sems(B.ss, B.rs)
     x, c = here.x, here.c
     vec = B.vb.at[0]
+    even = [sems.block(4) for _ in range(3)]
+    odd = [even[0], sems.block(4), even[2]]
 
     peers = [here.dev(c=1 - c), here.dev(h=1 - here.h), here.dev(x=1 - x)]
     for axis in ("y", "z"):
@@ -517,7 +514,7 @@
         B.normed[rows32(i)] = (n * gain + shift).astype(BF)
         return carry
 
-    lax.fori_loop(0, 8, norm_block, 0)
+    lax.fori_loop(0, 8, norm_block, 0, unroll=2)
     for cp in heads:
         cp.wait()
     qv_bias = B.qv_bias[...].astype(F32)
@@ -540,7 +537,7 @@
     B.mixed[...] = mixed.astype(BF)
 
     pl.semaphore_wait(bar, len(peers))
-    branch = TensorSum(here, sems, B.pa, B.lca, B.lxa.at[0], B.hidden)
+    branch = TensorSum(here, sems, B.pa, B.lca, B.lxa.at[0], B.hidden, even)
     branch.send(lambda n: nn(B.mixed[...], B.wout[:, COLS[n]]))
     slot_row = jnp.concatenate([B.slots[0, 0:1], B.slots[0, 1:2]], axis=1)
     slot_col = column(slot_row.astype(F32))
@@ -571,7 +568,7 @@
         B.gating[rows] = sig * B.valid[rows]
         return carry + fold(h * h * B.valid[rows])
 
-    stat(0, total(lax.fori_loop(0, 8, hidden_block, jnp.zeros((8, 1024), F32))))
+    stat(0, total(lax.fori_loop(0, 8, hidden_block, jnp.zeros((8, 1024), F32), unroll=2)))
     for n in range(4):
         B.rows0[:, COLS[n]] = pick(B.hot_s[...], B.hidden[:, COLS[n]])
     ffn_gain = B.ffn_gain[...].astype(F32)
@@ -589,7 +586,7 @@
                 low_ref[rows] = (n * g + s).astype(BF)
                 return carry
 
-            lax.fori_loop(0, 4, block, 0)
+            lax.fori_loop(0, 4, block, 0, unroll=2)
 
     def gelu_parts(v):
         t = jnp.tanh(ROOT * (v + 0.044715 * (v * v * v)))
@@ -619,7 +616,7 @@
 
         return make
 
-    first = TensorSum(here, sems, B.pa, B.lca, B.lxa.at[1], B.rows1)
+    first = TensorSum(here, sems, B.pa, B.lca, B.lxa.at[1], B.rows1, odd)
     first.send(down(B.act0))
     experts = fetch_experts(1)
     m0w = Moved(here, "b", 256, B.ys, B.gy0, sems).start(B.act0)
@@ -654,7 +651,7 @@
             B.rows1[rows] = r1
             return carry + fold(r1 * r1 * B.filled[rows])
 
-        sq = lax.fori_loop(0, 4, rows1_block, sq)
+        sq = lax.fori_loop(0, 4, rows1_block, sq, unroll=2)
     stat(1, total(sq))
     expert_norm(B.rows1, B.n1, 1)
     s1u = Shared(here, "a", B.gs1u, sems).start(B.n1)
@@ -675,10 +672,10 @@
 
         return make
 
-    back1 = TensorSum(here, sems, B.pa, B.lca, B.lxa.at[0], B.gwork)
+    back1 = TensorSum(here, sems, B.pa, B.lca, B.lxa.at[0], B.gwork, even)
     back1.send(normed_grad(B.gp1))
     m1u = Moved(here, "a", 0, B.ys, B.gy1, sems).start(B.gp1)
-    second = TensorSum(here, sems, B.pb, B.lcb, B.lxb, B.rows2)
+    second = TensorSum(here, sems, B.pb, B.lcb, B.lxb, B.rows2, [sems.block(4) for _ in range(3)])
     second.send(down(B.act1))
     experts = fetch_experts(0)
     m0w.sent()
@@ -703,7 +700,7 @@
                 return tuple(out)
 
             zero = jnp.zeros((8, 1024), F32)
-            sums = lax.fori_loop(0, 4, block, (zero,) * (2 if go_ref is None else 3))
+            sums = lax.fori_loop(0, 4, block, (zero,) * (2 if go_ref is None else 3), unroll=2)
             at = e * 2 + j
             vec[GAIN + at : GAIN + at + 1] = down_rows(sums[0])
             vec[SHIFT + at : SHIFT + at + 1] = down_rows(sums[1])
@@ -720,7 +717,7 @@
             gp = (ga * B.slope0[half(e), COLS[n]]).astype(BF)
             B.gp0[half(e), COLS[n]] = gp
             vec[UP_B + e * 2 : UP_B + e * 2 + 1, COLS[n]] = down_rows(gp.astype(F32))
-    back0 = TensorSum(here, sems, B.pa, B.lca, B.lxa.at[1], B.gwork)
+    back0 = TensorSum(here, sems, B.pa, B.lca, B.lxa.at[1], B.gwork, odd)
     back0.send(normed_grad(B.gp0))
     state = {}
     def slot_gates():
@@ -767,7 +764,7 @@
                 B.rows2[rows] = r2
                 return carry + fold(r2 * r2 * B.filled[rows])
 
-            sq = lax.fori_loop(0, 4, rows2_block, sq)
+            sq = lax.fori_loop(0, 4, rows2_block, sq, unroll=2)
         stat(2, total(sq))
         gate_grad = jnp.zeros((256, 1), F32)
         result_sq = jnp.zeros((256, 1), F32)
@@ -791,7 +788,7 @@
             )
 
         zero = jnp.zeros((8, 1024), F32)
-        sums = lax.fori_loop(0, 8, gate_block, (zero, zero))
+        sums = lax.fori_loop(0, 8, gate_block, (zero, zero), unroll=2)
         for e in range(2):
             vec[CENT + e : CENT + e + 1] = down_rows(sums[e])
         for k, axis in enumerate(("b", "a")):
@@ -824,7 +821,7 @@
         B.gv[...] = gv.astype(BF)
         vec[QV_B : QV_B + 1, 0:256] = down_rows(B.gq[...].astype(F32))
         vec[QV_B : QV_B + 1, 256:512] = down_rows(B.gv[...].astype(F32))
-        state["back"] = back = TensorSum(here, sems, B.pa, B.lca, B.lxa.at[0], B.gwork)
+        state["back"] = back = TensorSum(here, sems, B.pa, B.lca, B.lxa.at[0], B.gwork, even)
         grads = (B.gq, B.gk, B.gv)
         back.send(lambda n: sum(nt(grads[s][...], B.wqkv[s, COLS[n], :]) for s in range(3)))
 
@@ -866,7 +863,7 @@
             B.tokens_grad[rows] = (B.ghidden[rows] + unit_back(gn, gain, n, r)).astype(BF)
             return carry[0] + fold(gn * n), carry[1] + fold(gn)
 
-        sums = lax.fori_loop(0, 8, last_block, (zero, zero))
+        sums = lax.fori_loop(0, 8, last_block, (zero, zero), unroll=2)
         vec[LN_GAIN : LN_GAIN + 1] = down_rows(sums[0])
         vec[LN_SHIFT : LN_SHIFT + 1] = down_rows(sums[1])
         gather.ring_y()
@@ -895,38 +892,56 @@
             B.qkv_grad[2] = mine[:, :256]
             B.out_grad[...] = mine[:, 256:]
 
-    steps = {
-        "n1_relay": s1u.relay,
-        "gp0": move_gp0,
-        "rows2": second.end,
-        "result": result,
-        "go0_relay": s0w.relay,
-        "back0_end": back0.end,
-        "attention": attention_back,
-        "tokens": tokens_back,
-        "sums_z": gather.ring_z,
-        "sums_x": gather.pair,
-        "sums_out": lambda: gather.finish(B.sums),
-    }
-    for n in range(3):
-        steps[f"back0_{n}"] = lambda n=n: back0.third(n)
-        steps[f"back_{n}"] = lambda n=n: state["back"].third(n)
-    for m in range(2):
-        for j, g in ((1, eg1[m]), (0, eg0[m])):
-            at = f"{j}{m}"
-            steps["mul" + at] = g.multiply if j else lambda m=m: first_sublayer(m)
-            steps["mid" + at] = g.ring.middle
-            steps["x" + at] = g.across
-            steps["spread" + at] = g.spread
-            steps["out" + at] = lambda g=g, m=m, j=j: g.finish((B.up_grad, B.down_grad)[m], j)
-        steps[f"attn{m}"] = lambda m=m: attention_grads(m)
-        steps[f"attn_mid{m}"] = lambda m=m: rings[m].middle()
-        steps[f"attn_next{m}"] = lambda m=m: second_ring(m)
-        steps[f"attn_mid_next{m}"] = lambda m=m: rings2[m].middle()
-        steps[f"attn_x{m}"] = lambda m=m: attention_swap(m)
-        steps[f"attn_out{m}"] = lambda m=m: attention_out(m)
-    for name in ORDER:
-        steps[name]()
+    s1u.relay()
+    move_gp0()
+    eg1[0].multiply()
+    back0.third(0)
+    s0w.relay()
+    eg1[1].multiply()
+    second.end()
+    result()
+    first_sublayer(0)
+    back0.third(1)
+    first_sublayer(1)
+    back0.third(2)
+    back0.end()
+    attention_back()
+    eg1[0].ring.middle()
+    eg0[0].ring.middle()
+    eg1[1].ring.middle()
+    eg1[0].across()
+    state["back"].third(0)
+    eg0[1].ring.middle()
+    state["back"].third(1)
+    attention_grads(1)
+    eg0[1].across()
+    state["back"].third(2)
+    tokens_back()
+    rings[1].middle()
+    eg1[1].across()
+    attention_grads(0)
+    eg0[0].across()
+    gather.ring_z()
+    rings[0].middle()
+    second_ring(1)
+    eg0[1].spread()
+    second_ring(0)
+    rings2[1].middle()
+    gather.pair()
+    eg1[1].spread()
+    rings2[0].middle()
+    eg0[0].spread()
+    eg1[0].spread()
+    gather.finish(B.sums)
+    attention_swap(1)
+    attention_swap(0)
+    eg0[0].finish((B.up_grad, B.down_grad)[0], 0)
+    eg0[1].finish((B.up_grad, B.down_grad)[1], 0)
+    attention_out(1)
+    eg1[0].finish((B.up_grad, B.down_grad)[0], 1)
+    eg1[1].finish((B.up_grad, B.down_grad)[1], 1)
+    attention_out(0)
+    assert sems.n == N_SEMS, sems.n
     for job in (s0u, s0w, gather, *rings.values(), *rings2.values()):
         job.done()
     for cp in [*swaps.values(), *gate_cps]:

time: 178 us -> 170 us (0.955)
  Pallas kernels: 176 us -> 168 us
    pallas_call x1, Pallas kernels: 172 us -> 165 us  [local(): pl.pallas_call(layer_kernel, out_shape=tuple((jax.ShapeDtypeStruct(*spec)...]
where the time goes in v4:
time: 170 us; the launch traced here: 169 us
  Pallas kernels  168 us (99%)
    pallas_call x1, Pallas kernels, local(): pl.pallas_call(layer_kernel, out_shape=tuple((jax.ShapeDtypeStruct(*spec)...  165 us
    pallas_call x1, Pallas kernels, local(): pl.pallas_call(finish_kernel, out_shape=tuple((jax.ShapeDtypeStruct(a.sha...  3.62 us

profile of v4, /device:TPU:1, one launch (start us, length us, event | category | flops | bytes accessed | tf_op | source)
XLA Modules:
  0.0 169.0 jit_solution(5176516926581554339)
XLA Ops:
  0.7 164.6 %shard_map.297 = (bf16[256,1024]{1,0:T(8,128)(2,1)}, bf16[256,1024]{1,0:T(8,128)(2,1)}, f32[3,32,256]{2,1,0:T(8,128)}, f32[32,256]{1,0:T(8,128)}, f32[2,2,32,102...) custom-call(bf16[256,1024]{1,0:T(8,128)(2,1)} %refs_0_.1, s32[1,256]{1,0:T(1,128)} %bitcast.8, ...), custom_call_target="tpu_custom_call" | custom-call | tf_op jit(solution)/shard_map/pallas_call | solution.py:988
  165.2 3.6 %shard_map.298 = (bf16[256,1024]{1,0:T(8,128)(2,1)}, bf16[256,1024]{1,0:T(8,128)(2,1)}, f32[3,32,256]{2,1,0:T(8,128)}, f32[32,256]{1,0:T(8,128)}, f32[2,2,32,102...) custom-call(bf16[256,1024]{1,0:T(8,128)(2,1)} %get-tuple-element.39., ...), custom_call_target="tpu_custom_call" | custom-call | tf_op jit(solution)/shard_map/pallas_call | solution.py:1009

commit v5 on v4

--- a/solution.py
+++ b/solution.py
@@ -43,6 +43,10 @@
         on_y = {"y": 1, "z": 0, "a": 1 - self.c, "b": self.c}[axis]
         y, z = (self.y + step * on_y) % 4, (self.z + step * (1 - on_y)) % 4
         return self.dev(y=y, z=z, c=c)
+
+
+def here_not(flag):
+    return not flag if isinstance(flag, bool) else jnp.logical_not(flag)
 
 
 class Sems:
@@ -355,6 +359,7 @@
     "tok", "seg", "routes", "slots", "ln_gain", "ln_shift", "qkv_w", "qv_bias", "out_w", "out_bias",
     "cent", "ffn_gain", "ffn_shift", "up_w", "up_bias", "down_w", "down_bias", "cot",
 )
+OUT_HBM = ("result", "tokens_grad")
 IN_HBM = ("up_w", "down_w", "qkv_w", "out_w")
 OUTPUTS = {
     "result": ((256, 1024), BF),
@@ -388,11 +393,122 @@
     "partu": PART, "partw": PART,
     "l1": ((2, 2, 128, 512), F32), "l2": ((2, 2, 256, 512), F32),
     "lx": ((2, 2, 128, 512), F32), "gates": ((4, 8, 128), F32), "land": ((2, 2, 4, 2, 32, 256), F32),
-    "a1": ((2, 2, 128, 512), F32), "a2": ((2, 2, 256, 512), F32),
-    "b1": ((2, 2, 32, 512), F32), "b2": ((2, 2, 64, 512), F32), "ax": ((2, 32, 512), F32),
-    "vb": ((11, 24, 1024), F32),
+    "a1": ((2, 2, 128, 384), F32), "a2": ((2, 2, 256, 384), F32),
+    "b1": ((2, 32, 256), F32), "b2": ((2, 64, 256), F32), "ax": ((32, 256), F32),
+    "gsn": PART, "gyn": ((512, 384), F32), "lxn": ((128, 384), F32), "landn": ((2, 2, 32, 384), F32),
+    "vb": ((10, 24, 1024), F32), "low_out": LOW,
 }
 N_SEMS = 116
+
+
+class QkvGrads:
+    def __init__(self, here, shared, ys, gy, right, part, l1, l2, lx, land, sems):
+        self.here, self.shared, self.ys, self.gy, self.right = here, shared, ys, gy, right
+        self.part, self.lx, self.land, self.sems = part, lx, land, sems
+        self.ring = RingSum(here, "b", part, 0, 256, l1, l2, sems)
+        self.stays = here.a // 2 == here.c
+
+    def move(self, grads):
+        here, ys, gy, c = self.here, self.ys, self.gy, self.here.c
+        for n, g in enumerate(grads):
+            ys[:, COLS[n]] = g[...].astype(F32)
+        self.k = self.sems.block(1)
+        for dc in range(2):
+            axis, e = "ab"[dc], (c + dc) % 2
+            p = getattr(here, axis)
+            spot = gy.at[pl.ds(pl.multiple_of(p * 128, 128), 128)]
+            for q in range(2):
+                to = 2 * c + q
+                block = ys.at[
+                    pl.ds(pl.multiple_of(e * 128, 128), 128), q * 384 : q * 384 + 384
+                ]
+
+                def send(block=block, spot=spot, to=to, axis=axis, e=e, p=p):
+                    self.sems.copy(block, spot, here.ring(axis, to - p + 4, c=e), self.k)
+
+                if dc:
+                    send()
+                    continue
+
+                def keep(block=block, spot=spot):
+                    spot[...] = block[...]
+
+                pl.when(to == p)(keep)
+                pl.when(to != p)(send)
+
+    def settle(self, wait, rows):
+        view = self.gy
+        pl.when(self.stays)(lambda: wait(view.at[pl.ds(0, 3 * rows)]))
+        pl.when(here_not(self.stays))(lambda: wait(view.at[pl.ds(0, 4 * rows)]))
+
+    def multiply(self):
+        self.shared.arrive()
+        self.settle(lambda view: self.sems.all_recv(self.k, view), 128)
+        self.right[:, 0:384] = self.gy[...].astype(BF)
+        c = self.here.c
+        per_y, per_z = 32 + 224 * c, 256 - 224 * c
+
+        def block(k, carry):
+            lanes = pl.ds(pl.multiple_of((k % 4) * 128, 128), 128)
+            left = [
+                self.shared.buf[
+                    pl.ds(pl.multiple_of(p * 256 + (k // 4) * 128, 128), 128), lanes
+                ].astype(BF)
+                for p in range(4)
+            ]
+            res = tn(jnp.concatenate(left, axis=0), self.right[:, 0:384])
+            for z in range(4):
+                at = (k // 4) * 128 + (k % 4) * per_y + z * per_z
+                self.part[pl.ds(pl.multiple_of(at, 32), 32)] = res[z * 32 : z * 32 + 32]
+            return carry
+
+        lax.fori_loop(0, 8, block, 0)
+        self.ring.start()
+
+    def across(self):
+        here = self.here
+        self.ring.arrive()
+        away = pl.multiple_of(self.ring.p * 256 + (1 - here.x) * 128, 128)
+        self.swap = self.sems.copy(self.part.at[pl.ds(away, 128)], self.lx, here.dev(x=1 - here.x))
+
+    def spread(self):
+        here = self.here
+        self.swap.wait_recv()
+        base = self.ring.p * 256 + here.x * 128
+        mine = pl.ds(pl.multiple_of(base, 128), 128)
+        self.part[mine] = self.part[mine] + self.lx[...]
+        self.k2 = self.sems.block(1)
+        p, owner = here.a, here.a // 2
+        spot = self.land.at[p % 2, here.c]
+        for step in (1, 3, 2, 0):
+            block = self.part.at[pl.ds(pl.multiple_of(base + ((p + step) % 4) * 32, 32), 32)]
+
+            def send(block=block, step=step):
+                self.sems.copy(block, spot, here.ring("a", step, c=owner), self.k2)
+
+            if step:
+                send()
+                continue
+
+            def keep(block=block):
+                spot[...] = block[...]
+
+            pl.when(self.stays)(keep)
+            pl.when(here_not(self.stays))(send)
+
+    def finish(self, out):
+        self.settle(lambda view: self.sems.all_recv(self.k2, view), 32)
+        left, right = (self.land[half, 0] + self.land[half, 1] for half in range(2))
+        out[0] = left[:, 0:256]
+        out[1, :, 0:128] = left[:, 256:384]
+        out[1, :, 128:256] = right[:, 0:128]
+        out[2] = right[:, 128:384]
+
+    def done(self):
+        self.settle(lambda view: self.sems.all_sent(self.k, view), 128)
+        self.settle(lambda view: self.sems.all_sent(self.k2, view), 32)
+        self.swap.wait_send()
+        self.ring.done()
 
 
 class Totals:
@@ -421,12 +537,12 @@
         self.send(at, at, [self.here.ring("z", step) for step in (1, 3, 2)])
 
     def pair(self):
-        self.buf[9] = self.four(5)
-        self.send(9, 10, [self.here.dev(x=1 - self.here.x)])
+        self.buf[0] = self.four(5)
+        self.send(0, 9, [self.here.dev(x=1 - self.here.x)])
 
     def finish(self, out):
         self.wait[0].wait_recv()
-        out[...] = self.buf[9] + self.buf[10]
+        out[...] = self.buf[0] + self.buf[9]
 
     def done(self):
         for cp in self.cps:
@@ -537,6 +653,7 @@
     B.mixed[...] = mixed.astype(BF)
 
     pl.semaphore_wait(bar, len(peers))
+    sn = Shared(here, "a", B.gsn, sems).start(B.normed)
     branch = TensorSum(here, sems, B.pa, B.lca, B.lxa.at[0], B.hidden, even)
     branch.send(lambda n: nn(B.mixed[...], B.wout[:, COLS[n]]))
     slot_row = jnp.concatenate([B.slots[0, 0:1], B.slots[0, 1:2]], axis=1)
@@ -551,6 +668,8 @@
     stat(4, total(B.valid[...]))
     for n in range(2):
         branch.third(n)
+    sn.relay()
+    branch.third(2)
     s1w.relay()
     branch.end()
 
@@ -743,9 +862,12 @@
                     B.lx.at[1, m], B.land.at[1, m], sems)
         for m in range(2)
     ]
-    lefts = (B.normed, B.normed, B.normed, B.gbranch)
-    rights = (B.gq, B.gk, B.gv, B.mixed)
-    apart = (B.gs1u, B.gs1w)
+    low, few = pl.ds(0, 256), pl.ds(0, 384)
+    apart = (None, B.gs1w.at[:, low])
+    qkv = QkvGrads(
+        here, sn, B.rows0, B.gyn, B.right, B.gs1u.at[:, few],
+        two(B.a1.at[0]), two(B.a2.at[0]), B.lxn, B.landn, sems,
+    )
     rings, rings2, swaps = {}, {}, {}
     gather = Totals(here, B.vb, sems)
 
@@ -771,9 +893,11 @@
         for n in range(4):
             comb = pick(B.hot_t[...], B.rows2[:, COLS[n]])
             res = B.hidden[:, COLS[n]] + B.gating[...] * comb
-            B.result[:, COLS[n]] = res.astype(BF)
+            B.low_out[:, COLS[n]] = res.astype(BF)
             result_sq = result_sq + jnp.sum(res * res, axis=-1, keepdims=True)
             gate_grad = gate_grad + jnp.sum(B.cot[:, COLS[n]].astype(F32) * comb, axis=-1, keepdims=True)
+        state["out"] = pltpu.make_async_copy(B.low_out, B.result, B.ws.at[0])
+        state["out"].start()
         stat(3, total(result_sq * B.valid[...]))
         B.gating[...] = gate_grad * B.sig[...] * (1.0 - B.sig[...]) * B.valid[...]
 
@@ -833,45 +957,51 @@
         pl.semaphore_wait(B.free.at[m], 2)
         eg0[m].multiply()
 
+    def qkv_multiply():
+        s1u.done()
+        qkv.multiply()
+
     def attention_grads(m):
-        (s1u, s1w)[m].done()
+        s1w.done()
         last_y = (m + c) % 2
-        for j in range(2):
-
-            def block(k, carry, m=m, last_y=last_y, left=lefts[2 * m + j], right=rights[2 * m + j], j=j):
-                lanes = pl.ds(pl.multiple_of(k * 128, 128), 128)
-                res = tn(left[:, lanes], right[...])
-                for z in range(4):
-                    at = (k // 4) * 32 + (k % 4) * (256 - 192 * last_y) + z * (64 + 192 * last_y)
-                    apart[m][pl.ds(pl.multiple_of(at, 32), 32), j * 256 : j * 256 + 256] = res[
-                        z * 32 : z * 32 + 32
-                    ]
-                return carry
-
-            lax.fori_loop(0, 8, block, 0)
-        rings[m] = RingSum(here, "ab"[m], apart[m], 0, 256, two(B.a1.at[m]), two(B.a2.at[m]), sems)
+
+        def block(k, carry):
+            lanes = pl.ds(pl.multiple_of(k * 128, 128), 128)
+            res = tn(B.gbranch[:, lanes], B.mixed[...])
+            for z in range(4):
+                at = (k // 4) * 32 + (k % 4) * (256 - 192 * last_y) + z * (64 + 192 * last_y)
+                apart[m][pl.ds(pl.multiple_of(at, 32), 32)] = res[z * 32 : z * 32 + 32]
+            return carry
+
+        lax.fori_loop(0, 8, block, 0)
+        l1 = [B.a1.at[m, k, :, low] for k in range(2)]
+        l2 = [B.a2.at[m, k, :, low] for k in range(2)]
+        rings[m] = RingSum(here, "ab"[m], apart[m], 0, 256, l1, l2, sems)
         rings[m].start()
 
     def tokens_back():
         state["back"].end()
+        state["out"].wait()
         zero = jnp.zeros((8, 1024), F32)
 
         def last_block(i, carry):
             rows = rows32(i)
             n, r = unit(B.tok[rows].astype(F32))
             gn = B.gwork[rows]
-            B.tokens_grad[rows] = (B.ghidden[rows] + unit_back(gn, gain, n, r)).astype(BF)
+            B.low_out[rows] = (B.ghidden[rows] + unit_back(gn, gain, n, r)).astype(BF)
             return carry[0] + fold(gn * n), carry[1] + fold(gn)
 
         sums = lax.fori_loop(0, 8, last_block, (zero, zero), unroll=2)
         vec[LN_GAIN : LN_GAIN + 1] = down_rows(sums[0])
         vec[LN_SHIFT : LN_SHIFT + 1] = down_rows(sums[1])
+        state["out"] = pltpu.make_async_copy(B.low_out, B.tokens_grad, B.ws.at[0])
+        state["out"].start()
         gather.ring_y()
 
     def second_ring(m):
         rings[m].arrive()
         base = rings[m].p * 256
-        b1, b2 = two(B.b1.at[m]), two(B.b2.at[m])
+        b1, b2 = two(B.b1), two(B.b2)
         rings2[m] = RingSum(here, "ba"[m], apart[m], base, 64, b1, b2, sems)
         rings2[m].start()
 
@@ -879,70 +1009,65 @@
         rings2[m].arrive()
         base = rings2[m].base + rings2[m].p * 64
         away = pl.ds(pl.multiple_of(base + (1 - x) * 32, 32), 32)
-        swaps[m] = sems.copy(apart[m].at[away], B.ax.at[m], here.dev(x=1 - x))
+        swaps[m] = sems.copy(apart[m].at[away], B.ax, here.dev(x=1 - x))
 
     def attention_out(m):
         swaps[m].wait_recv()
         base = rings2[m].base + rings2[m].p * 64
-        mine = apart[m][pl.ds(pl.multiple_of(base + x * 32, 32), 32)] + B.ax[m]
-        if m == 0:
-            B.qkv_grad[0] = mine[:, :256]
-            B.qkv_grad[1] = mine[:, 256:]
-        else:
-            B.qkv_grad[2] = mine[:, :256]
-            B.out_grad[...] = mine[:, 256:]
+        B.out_grad[...] = apart[m][pl.ds(pl.multiple_of(base + x * 32, 32), 32)] + B.ax[...]
 
     s1u.relay()
     move_gp0()
+    s0w.relay()
+    second.end()
+    eg1[1].multiply()
+    back0.third(0)
+    result()
+    back0.third(1)
+    back0.third(2)
     eg1[0].multiply()
-    back0.third(0)
-    s0w.relay()
-    eg1[1].multiply()
-    second.end()
-    result()
+    back0.end()
+    first_sublayer(1)
+    attention_back()
+    eg1[1].ring.middle()
     first_sublayer(0)
-    back0.third(1)
-    first_sublayer(1)
-    back0.third(2)
-    back0.end()
-    attention_back()
     eg1[0].ring.middle()
+    qkv.move((B.gq, B.gk, B.gv))
+    eg1[0].across()
     eg0[0].ring.middle()
-    eg1[1].ring.middle()
-    eg1[0].across()
+    eg1[1].across()
     state["back"].third(0)
-    eg0[1].ring.middle()
     state["back"].third(1)
-    attention_grads(1)
-    eg0[1].across()
     state["back"].third(2)
     tokens_back()
+    eg0[1].ring.middle()
+    qkv_multiply()
+    eg0[0].across()
+    attention_grads(1)
+    gather.ring_z()
+    qkv.ring.middle()
+    eg0[1].across()
     rings[1].middle()
-    eg1[1].across()
-    attention_grads(0)
-    eg0[0].across()
-    gather.ring_z()
-    rings[0].middle()
+    eg0[0].spread()
+    eg1[1].spread()
+    qkv.across()
     second_ring(1)
     eg0[1].spread()
-    second_ring(0)
+    gather.pair()
     rings2[1].middle()
-    gather.pair()
-    eg1[1].spread()
-    rings2[0].middle()
-    eg0[0].spread()
     eg1[0].spread()
+    eg0[0].finish((B.up_grad, B.down_grad)[0], 0)
+    qkv.spread()
+    attention_swap(1)
+    qkv.finish(B.qkv_grad)
+    eg1[0].finish((B.up_grad, B.down_grad)[0], 1)
+    attention_out(1)
+    eg0[1].finish((B.up_grad, B.down_grad)[1], 0)
     gather.finish(B.sums)
-    attention_swap(1)
-    attention_swap(0)
-    eg0[0].finish((B.up_grad, B.down_grad)[0], 0)
-    eg0[1].finish((B.up_grad, B.down_grad)[1], 0)
-    attention_out(1)
-    eg1[0].finish((B.up_grad, B.down_grad)[0], 1)
     eg1[1].finish((B.up_grad, B.down_grad)[1], 1)
-    attention_out(0)
+    state["out"].wait()
     assert sems.n == N_SEMS, sems.n
-    for job in (s0u, s0w, gather, *rings.values(), *rings2.values()):
+    for job in (sn, s0u, s0w, gather, qkv, *rings.values(), *rings2.values()):
         job.done()
     for cp in [*swaps.values(), *gate_cps]:
         cp.wait_send()
@@ -989,7 +1114,9 @@
         layer_kernel,
         out_shape=tuple(jax.ShapeDtypeStruct(*spec) for spec in OUTPUTS.values()),
         in_specs=in_specs,
-        out_specs=[pl.BlockSpec(memory_space=VM)] * len(OUTPUTS),
+        out_specs=[
+            pl.BlockSpec(memory_space=pl.ANY if name in OUT_HBM else VM) for name in OUTPUTS
+        ],
         scratch_shapes=[VM(*spec) for spec in SCRATCH.values()]
         + [pltpu.SemaphoreType.DMA((N_SEMS,)), pltpu.SemaphoreType.DMA((N_SEMS,)), pltpu.SemaphoreType.DMA((6,)), pltpu.SemaphoreType.REGULAR((2,))],
         compiler_params=pltpu.CompilerParams(

time: 170 us -> 163 us (0.959)
  Pallas kernels: 168 us -> 162 us
    pallas_call x1, Pallas kernels: 165 us -> 158 us  [local(): pl.pallas_call(layer_kernel, out_shape=tuple((jax.ShapeDtypeStruct(*spec)...]
where the time goes in v5:
time: 163 us; the launch traced here: 162 us
  Pallas kernels  162 us (99%)
    pallas_call x1, Pallas kernels, local(): pl.pallas_call(layer_kernel, out_shape=tuple((jax.ShapeDtypeStruct(*spec)...  158 us
    pallas_call x1, Pallas kernels, local(): pl.pallas_call(finish_kernel, out_shape=tuple((jax.ShapeDtypeStruct(a.sha...  3.62 us

profile of v5, /device:TPU:1, one launch (start us, length us, event | category | flops | bytes accessed | tf_op | source)
XLA Modules:
  0.0 162.5 jit_solution(3430217569572602513)
XLA Ops:
  0.7 158.0 %shard_map.297 = (bf16[256,1024]{1,0:T(8,128)(2,1)}, bf16[256,1024]{1,0:T(8,128)(2,1)}, f32[3,32,256]{2,1,0:T(8,128)}, f32[32,256]{1,0:T(8,128)}, f32[2,2,32,102...) custom-call(bf16[256,1024]{1,0:T(8,128)(2,1)} %refs_0_.1, s32[1,256]{1,0:T(1,128)} %bitcast.8, ...), custom_call_target="tpu_custom_call" | custom-call | tf_op jit(solution)/shard_map/pallas_call | solution.py:1113
  158.7 3.6 %shard_map.298 = (bf16[256,1024]{1,0:T(8,128)(2,1)}, bf16[256,1024]{1,0:T(8,128)(2,1)}, f32[3,32,256]{2,1,0:T(8,128)}, f32[32,256]{1,0:T(8,128)}, f32[2,2,32,102...) custom-call(bf16[256,1024]{1,0:T(8,128)(2,1)} %get-tuple-element.39., ...), custom_call_target="tpu_custom_call" | custom-call | tf_op jit(solution)/shard_map/pallas_call | solution.py:1136

commit v6 on v5

--- a/solution.py
+++ b/solution.py
@@ -1018,53 +1018,53 @@
 
     s1u.relay()
     move_gp0()
+    eg1[1].multiply()
+    second.end()
     s0w.relay()
-    second.end()
-    eg1[1].multiply()
     back0.third(0)
     result()
+    eg1[0].multiply()
     back0.third(1)
     back0.third(2)
-    eg1[0].multiply()
     back0.end()
+    first_sublayer(0)
+    eg1[1].ring.middle()
+    attention_back()
+    qkv.move((B.gq, B.gk, B.gv))
     first_sublayer(1)
-    attention_back()
-    eg1[1].ring.middle()
-    first_sublayer(0)
+    state["back"].third(0)
+    eg1[1].across()
+    state["back"].third(1)
+    eg0[0].ring.middle()
+    state["back"].third(2)
+    eg0[1].ring.middle()
+    tokens_back()
     eg1[0].ring.middle()
-    qkv.move((B.gq, B.gk, B.gv))
-    eg1[0].across()
-    eg0[0].ring.middle()
-    eg1[1].across()
-    state["back"].third(0)
-    state["back"].third(1)
-    state["back"].third(2)
-    tokens_back()
-    eg0[1].ring.middle()
     qkv_multiply()
     eg0[0].across()
     attention_grads(1)
+    eg0[1].across()
     gather.ring_z()
+    eg1[0].across()
     qkv.ring.middle()
-    eg0[1].across()
     rings[1].middle()
-    eg0[0].spread()
     eg1[1].spread()
     qkv.across()
+    eg0[0].spread()
     second_ring(1)
+    eg1[0].spread()
+    rings2[1].middle()
     eg0[1].spread()
     gather.pair()
-    rings2[1].middle()
-    eg1[0].spread()
     eg0[0].finish((B.up_grad, B.down_grad)[0], 0)
     qkv.spread()
     attention_swap(1)
+    attention_out(1)
     qkv.finish(B.qkv_grad)
-    eg1[0].finish((B.up_grad, B.down_grad)[0], 1)
-    attention_out(1)
-    eg0[1].finish((B.up_grad, B.down_grad)[1], 0)
     gather.finish(B.sums)
     eg1[1].finish((B.up_grad, B.down_grad)[1], 1)
+    eg0[1].finish((B.up_grad, B.down_grad)[1], 0)
+    eg1[0].finish((B.up_grad, B.down_grad)[0], 1)
     state["out"].wait()
     assert sems.n == N_SEMS, sems.n
     for job in (sn, s0u, s0w, gather, qkv, *rings.values(), *rings2.values()):

time: 163 us -> 158 us (0.969)
  Pallas kernels: 162 us -> 157 us
    pallas_call x1, Pallas kernels: 158 us -> 153 us  [local(): pl.pallas_call(layer_kernel, out_shape=tuple((jax.ShapeDtypeStruct(*spec)...]
where the time goes in v6:
time: 158 us
  Pallas kernels  157 us (99%)
    pallas_call x1, Pallas kernels, local(): pl.pallas_call(layer_kernel, out_shape=tuple((jax.ShapeDtypeStruct(*spec)...  153 us
    pallas_call x1, Pallas kernels, local(): pl.pallas_call(finish_kernel, out_shape=tuple((jax.ShapeDtypeStruct(a.sha...  3.62 us

profile of v6, /device:TPU:1, one launch (start us, length us, event | category | flops | bytes accessed | tf_op | source)
XLA Modules:
  0.0 157.8 jit_solution(13274013470126471761)
XLA Ops:
  0.7 153.4 %shard_map.297 = (bf16[256,1024]{1,0:T(8,128)(2,1)}, bf16[256,1024]{1,0:T(8,128)(2,1)}, f32[3,32,256]{2,1,0:T(8,128)}, f32[32,256]{1,0:T(8,128)}, f32[2,2,32,102...) custom-call(bf16[256,1024]{1,0:T(8,128)(2,1)} %refs_0_.1, s32[1,256]{1,0:T(1,128)} %bitcast.8, ...), custom_call_target="tpu_custom_call" | custom-call | tf_op jit(solution)/shard_map/pallas_call | solution.py:1113
  154.1 3.6 %shard_map.298 = (bf16[256,1024]{1,0:T(8,128)(2,1)}, bf16[256,1024]{1,0:T(8,128)(2,1)}, f32[3,32,256]{2,1,0:T(8,128)}, f32[32,256]{1,0:T(8,128)}, f32[2,2,32,102...) custom-call(bf16[256,1024]{1,0:T(8,128)(2,1)} %get-tuple-element.39., ...), custom_call_target="tpu_custom_call" | custom-call | tf_op jit(solution)/shard_map/pallas_call | solution.py:1136

commit v7 on v5

--- a/solution.py
+++ b/solution.py
@@ -1017,54 +1017,54 @@
         B.out_grad[...] = apart[m][pl.ds(pl.multiple_of(base + x * 32, 32), 32)] + B.ax[...]
 
     s1u.relay()
-    move_gp0()
     s0w.relay()
-    second.end()
     eg1[1].multiply()
     back0.third(0)
+    eg1[0].multiply()
+    move_gp0()
+    second.end()
     result()
     back0.third(1)
+    first_sublayer(1)
+    eg1[0].ring.middle()
+    eg1[1].ring.middle()
     back0.third(2)
-    eg1[0].multiply()
     back0.end()
-    first_sublayer(1)
     attention_back()
-    eg1[1].ring.middle()
     first_sublayer(0)
-    eg1[0].ring.middle()
     qkv.move((B.gq, B.gk, B.gv))
     eg1[0].across()
-    eg0[0].ring.middle()
-    eg1[1].across()
     state["back"].third(0)
     state["back"].third(1)
+    eg1[1].across()
     state["back"].third(2)
+    eg0[1].ring.middle()
     tokens_back()
-    eg0[1].ring.middle()
+    eg0[0].ring.middle()
     qkv_multiply()
-    eg0[0].across()
+    eg0[1].across()
     attention_grads(1)
     gather.ring_z()
+    eg0[0].across()
     qkv.ring.middle()
-    eg0[1].across()
     rings[1].middle()
-    eg0[0].spread()
     eg1[1].spread()
+    eg0[1].spread()
     qkv.across()
     second_ring(1)
-    eg0[1].spread()
+    eg1[0].spread()
+    eg1[1].finish((B.up_grad, B.down_grad)[1], 1)
     gather.pair()
     rings2[1].middle()
-    eg1[0].spread()
-    eg0[0].finish((B.up_grad, B.down_grad)[0], 0)
+    eg0[0].spread()
+    eg1[0].finish((B.up_grad, B.down_grad)[0], 1)
     qkv.spread()
+    eg0[1].finish((B.up_grad, B.down_grad)[1], 0)
     attention_swap(1)
     qkv.finish(B.qkv_grad)
-    eg1[0].finish((B.up_grad, B.down_grad)[0], 1)
+    eg0[0].finish((B.up_grad, B.down_grad)[0], 0)
+    gather.finish(B.sums)
     attention_out(1)
-    eg0[1].finish((B.up_grad, B.down_grad)[1], 0)
-    gather.finish(B.sums)
-    eg1[1].finish((B.up_grad, B.down_grad)[1], 1)
     state["out"].wait()
     assert sems.n == N_SEMS, sems.n
     for job in (sn, s0u, s0w, gather, qkv, *rings.values(), *rings2.values()):

time: 163 us -> 161 us (0.988)
  Pallas kernels: 162 us -> 160 us
where the time goes in v7:
time: 161 us
  Pallas kernels  160 us (99%)
    pallas_call x1, Pallas kernels, local(): pl.pallas_call(layer_kernel, out_shape=tuple((jax.ShapeDtypeStruct(*spec)...  156 us
    pallas_call x1, Pallas kernels, local(): pl.pallas_call(finish_kernel, out_shape=tuple((jax.ShapeDtypeStruct(a.sha...  3.62 us

profile of v7, /device:TPU:1, one launch (start us, length us, event | category | flops | bytes accessed | tf_op | source)
XLA Modules:
  0.0 160.8 jit_solution(17307084936681214038)
XLA Ops:
  0.7 156.4 %shard_map.297 = (bf16[256,1024]{1,0:T(8,128)(2,1)}, bf16[256,1024]{1,0:T(8,128)(2,1)}, f32[3,32,256]{2,1,0:T(8,128)}, f32[32,256]{1,0:T(8,128)}, f32[2,2,32,102...) custom-call(bf16[256,1024]{1,0:T(8,128)(2,1)} %refs_0_.1, s32[1,256]{1,0:T(1,128)} %bitcast.8, ...), custom_call_target="tpu_custom_call" | custom-call | tf_op jit(solution)/shard_map/pallas_call | solution.py:1113
  157.1 3.6 %shard_map.298 = (bf16[256,1024]{1,0:T(8,128)(2,1)}, bf16[256,1024]{1,0:T(8,128)(2,1)}, f32[3,32,256]{2,1,0:T(8,128)}, f32[32,256]{1,0:T(8,128)}, f32[2,2,32,102...) custom-call(bf16[256,1024]{1,0:T(8,128)(2,1)} %get-tuple-element.39., ...), custom_call_target="tpu_custom_call" | custom-call | tf_op jit(solution)/shard_map/pallas_call | solution.py:1136
